TPU v7x, 256 devices: a whole 4x4x8 slice. The times are simulated.
256 devices in a mesh: seq: 32 (over z, x), head: 8 (over y, core).
Axes of the slice: x: 4, y: 4, z: 8, core: 2. Of those that a mesh axis runs over, the one named last changes fastest.
Arguments:
- mixer_input: bfloat16 [65536, 5120], P('seq', 'head'), may hold values from -6 to 6
- write_rows: bfloat16 [65536, 128], P(('seq', 'head')), may hold values from -1.796875 to 1.796875
- read_rows: bfloat16 [65536, 128], P(('seq', 'head')), may hold values from -1.796875 to 1.796875
- log_decay: float32 [80, 65536], P('head', 'seq'), may hold values from -2 to 0, as said below
- skip_gain: float32 [80], P('head'), may hold values from 0.25 to 1.75
- reset_offsets: int32 [32, 4], P('seq'), may hold values from 0 to 2048, as said below
- grad_out: bfloat16 [65536, 5120], P('seq', 'head'), may hold values from -6 to 6
Outputs:
- grad_input: bfloat16 [65536, 5120], P('seq', 'head')
- grad_write: float32 [65536, 128], P(('seq', 'head'))
- grad_read: float32 [65536, 128], P(('seq', 'head'))
Inputs may be any that keep to these rules, and one draw needn't show every extreme that they name: `log_decay`: every entry is negative. `reset_offsets`: row d lists, in increasing order, the offsets within block d of 2048 tokens at which an episode begins; unused slots hold 2048 and stand after the used ones; some row uses all 4 slots.
All inputs are finite; a program needn't handle non-finite values.
Results may differ from a plain program's by a relative error of at most 0.0055.
Values may be sent and summed in bfloat16 or wider, within the bound.
No kernel may reach another device: no remote copies, remote signals or barrier semaphores. Data moves between devices by JAX's collectives and lax.ppermute only.
A program may use at most 192 MiB of HBM per device.

v0:
```python
import jax
import jax.numpy as jnp
from jax import lax
from jax.sharding import PartitionSpec as P

SPAN = 256


def entering(part, axis, combine, identity, reverse):
    count = lax.axis_size(axis)
    place = lax.axis_index(axis)
    ahead = count - 1 - place if reverse else place
    gathered = jax.tree.map(lambda a: lax.all_gather(a, axis), part)
    state = jax.tree.map(lambda a, e: jnp.zeros_like(a) + jnp.asarray(e, a.dtype), part, identity)

    def one(step, state):
        source = count - 1 - step if reverse else step
        return combine(
            state, jax.tree.map(lambda a: lax.dynamic_index_in_dim(a, source, 0, False), gathered)
        )

    return lax.fori_loop(0, ahead, one, state)


def span_update(carry_state, inputs, skip_gain):
    feature_part, write_part, read_part, log_part, reset_part = inputs
    span_len = reset_part.shape[0]
    cum_log = jnp.cumsum(log_part, axis=1)
    reset_count = jnp.cumsum(reset_part)
    input_gain = jnp.sqrt(-jnp.expm1(2.0 * log_part))
    positions = jnp.arange(span_len)
    allowed = (positions[:, None] >= positions[None, :]) & (
        reset_count[:, None] == reset_count[None, :]
    )
    spread = cum_log[:, :, None] - cum_log[:, None, :]
    decay_matrix = jnp.exp(jnp.where(allowed[None], spread, -1e30))
    scores = jnp.dot(read_part, write_part.T, precision=lax.Precision.HIGHEST)
    weights = decay_matrix * scores[None] * input_gain[:, None, :]
    result = jnp.einsum("hts,shp->thp", weights, feature_part, precision=lax.Precision.HIGHEST)
    entry_decay = jnp.exp(cum_log) * (reset_count == 0)[None, :]
    carried = jnp.einsum("tn,hnp->thp", read_part, carry_state, precision=lax.Precision.HIGHEST)
    result = result + carried * entry_decay.T[:, :, None] + skip_gain[None, :, None] * feature_part
    tail_weight = (
        jnp.exp(cum_log[:, -1:] - cum_log) * (reset_count == reset_count[-1])[None, :] * input_gain
    )
    block_decay = jnp.exp(cum_log[:, -1]) * (reset_count[-1] == 0)
    fresh_state = jnp.einsum(
        "sn,shp->hnp",
        write_part,
        feature_part * tail_weight.T[:, :, None],
        precision=lax.Precision.HIGHEST,
    )
    return (block_decay[:, None, None] * carry_state + fresh_state, result)


def link_states(earlier, later):
    return (earlier[0] * later[0], later[0][:, None, None] * earlier[1] + later[1])


def shards(mixer_input, write_rows, read_rows, log_decay, skip_gain, reset_offsets, grad_out):
    write_whole, read_whole = (
        lax.all_gather(write_rows, "head", axis=0, tiled=True),
        lax.all_gather(read_rows, "head", axis=0, tiled=True),
    )
    token_count = mixer_input.shape[0]
    head_count = log_decay.shape[0]
    head_width = mixer_input.shape[1] // head_count
    feature_full = mixer_input.astype(jnp.float32).reshape(token_count, head_count, head_width)
    write_full = write_whole.astype(jnp.float32)
    read_full = read_whole.astype(jnp.float32)
    cotangent = grad_out.astype(jnp.float32).reshape(token_count, head_count, head_width)
    positions = jnp.arange(token_count, dtype=jnp.int32)
    resets = jnp.any(positions[:, None] == reset_offsets[0][None, :], axis=1).astype(jnp.float32)
    cum_log = jnp.cumsum(log_decay, axis=1)
    reset_count = jnp.cumsum(resets)
    input_gain = jnp.sqrt(-jnp.expm1(2.0 * log_decay))
    tail_weight = (
        jnp.exp(cum_log[:, -1:] - cum_log) * (reset_count == reset_count[-1])[None, :] * input_gain
    )
    local_state = jnp.einsum(
        "tn,thp->hnp",
        write_full,
        feature_full * tail_weight.T[:, :, None],
        precision=lax.Precision.HIGHEST,
    )
    block_decay = jnp.exp(cum_log[:, -1]) * (reset_count[-1] == 0)
    entry_decay = jnp.exp(cum_log) * (reset_count == 0)[None, :]
    local_grad = jnp.einsum(
        "tn,thp->hnp",
        read_full,
        cotangent * entry_decay.T[:, :, None],
        precision=lax.Precision.HIGHEST,
    )
    identity = (jnp.ones_like(block_decay), jnp.zeros_like(local_state))
    decay_before, state_in = entering(
        (block_decay, local_state), "seq", link_states, identity, False
    )
    decay_after, grad_in = entering((block_decay, local_grad), "seq", link_states, identity, True)
    spans = token_count // SPAN
    log_blocks = log_decay.reshape(head_count, spans, SPAN).transpose(1, 0, 2)
    reset_blocks = resets.reshape(spans, SPAN)

    def block_forward(feature_arg, write_arg, read_arg):
        feature_blocks = feature_arg.reshape(spans, SPAN, head_count, head_width)
        write_blocks = write_arg.reshape(spans, SPAN, write_arg.shape[1])
        read_blocks = read_arg.reshape(spans, SPAN, read_arg.shape[1])

        def advance(carry_state, inputs):
            return span_update(carry_state, inputs, skip_gain)

        end_state, outputs = lax.scan(
            advance, state_in, (feature_blocks, write_blocks, read_blocks, log_blocks, reset_blocks)
        )
        return (outputs.reshape(token_count, head_count, head_width), end_state)

    outputs, pullback = jax.vjp(block_forward, feature_full, write_full, read_full)
    grad_feature, grad_write_all, grad_read_all = pullback((cotangent, grad_in))
    grad_write, grad_read = (
        lax.psum_scatter(grad_write_all, "head", scatter_dimension=0, tiled=True),
        lax.psum_scatter(grad_read_all, "head", scatter_dimension=0, tiled=True),
    )
    grad_input = grad_feature.reshape(token_count, head_count * head_width).astype(jnp.bfloat16)
    return (grad_input, grad_write, grad_read)


def solution(mesh):
    in_specs = (
        P("seq", "head"),
        P(("seq", "head"), None),
        P(("seq", "head"), None),
        P("head", "seq"),
        P("head"),
        P("seq", None),
        P("seq", "head"),
    )
    out_specs = (P("seq", "head"), P(("seq", "head"), None), P(("seq", "head"), None))
    return jax.shard_map(shards, mesh=mesh, in_specs=in_specs, out_specs=out_specs, check_vma=False)
```

profile of v0, /device:TPU:1, one launch (start us, length us, event | category | flops | bytes accessed | tf_op | source)
XLA Modules:
  0.0 573.1 jit_solution(11024643300926106177)
XLA Ops:
  18.5 16.2 %all_gather.28 = bf16[2048,128]{1,0:T(8,128)(2,1)S(1)} all-gather(bf16[256,128]{1,0:T(8,128)(2,1)S(1)} %copy-done.5), channel_id=1, replica_groups=mesh['seq'=32,'head'=8] {'head'}, dimensions={0}, use_global_device_ids=true | all-gather | bytes 589824 | tf_op jit(solution)/shard_map/all_gather | solution.py:62
  35.7 3.3 fusion.90
  42.8 13.2 %all_gather.25 = bf16[2048,128]{1,0:T(8,128)(2,1)S(1)} all-gather(bf16[256,128]{1,0:T(8,128)(2,1)S(1)} %copy-done.6), channel_id=1, replica_groups=mesh['seq'=32,'head'=8] {'head'}, dimensions={0}, use_global_device_ids=true | all-gather | bytes 589824 | tf_op jit(solution)/shard_map/all_gather | solution.py:63
  56.1 3.3 fusion.87
  62.8 63.6 %all-reduce = f32[320]{0:T(512)S(1)} all-reduce(f32[320]{0:T(512)S(1)} %dynamic-update-slice), channel_id=2, replica_groups=mesh['seq'=32,'head'=8] {'seq'}, use_global_device_ids=true, to_apply=%add | all-reduce | flops 320 | bytes 2560
  126.5 5.0 copy.94
  131.5 3.9 copy.78
  136.6 7.4 %copy.95 = f32[80,8,8,256]{3,2,1,0:T(8,128)} copy(f32[80,8,8,256]{3,1,2,0:T(8,128)} %bitcast.375) | data formatting | bytes 10485760
  144.0 5.0 all-gather.8.cloned.1.call-done
  149.3 115.7 %while.83 = (s32[]{:T(128)}, f32[10,128,64]{1,2,0:T(8,128)S(1)}, f32[8,128,256]{1,2,0:T(8,128)}, f32[8,10,256,256]{3,2,1,0:T(8,128)}, f32[8,10,1,256]{3,1,2,0:T(...) while((s32[]{:T(128)}, f32[10,128,64]{1,2,0:T(8,128)S(1)}, ...), condition=%wide.region_14.15_spmd.clone.clone, body=%wide.region_9.14_spmd.clone.sunk.clone | while | flops 356031040 | bytes 10219655 | solution.py:111
  166.7 3.1 multiply_dynamic-update-slice_fusion.3
  265.1 45.4 %while.80 = (s32[]{:T(128)}, f32[10,128,64]{2,1,0:T(8,128)S(1)}, s32[]{:T(128)}, f32[32,10]{1,0:T(8,128)S(1)}, f32[32,10,128,64]{2,3,1,0:T(8,128)}) while((s32[]{:T(128)}, f32[10,128,64]{2,1,0:T(8,128)S(1)}, s32[]{:T(128)}, f32[32,10]{1,0:T(8,128)S(1)}, f32[32,10,128,64]{2,3,1,0:T(8,128)}) %tuple.184), condition=%wide.region_6.7_spmd.clone, body=%wide.region_5.6_spmd.sunk.clone | while | flops 163846 | bytes 2293995 | solution.py:22
  311.9 182.8 %while.82 = (s32[]{:T(128)}, f32[10,128,64]{1,2,0:T(8,128)S(1)}, bf16[8,256,10,64]{1,3,2,0:T(8,128)(2,1)}, f32[8,256,128]{2,1,0:T(8,128)S(1)}, f32[8,256,128]{2,...) while((s32[]{:T(128)}, f32[10,128,64]{1,2,0:T(8,128)S(1)}, ...), condition=%wide.region_17.18_spmd.clone, body=%wide.region_15.17_spmd.sunk.clone | while | flops 2217705472 | bytes 16956240 | solution.py:111
  316.4 4.2 fusion.184
  320.6 4.4 fusion.185
  339.3 4.2 fusion.184
  343.5 4.4 fusion.185
  362.1 4.2 fusion.184
  366.3 4.4 fusion.185
  385.0 4.2 fusion.184
  389.2 4.4 fusion.185
  407.8 4.2 fusion.184
  412.0 4.4 fusion.185
  430.7 4.2 fusion.184
  434.9 4.4 fusion.185
  453.5 4.2 fusion.184
  457.7 4.4 fusion.185
  476.4 4.2 fusion.184
  480.6 4.4 fusion.185
  496.3 3.4 copy.83
  503.2 27.1 %reduce-scatter.3.cloned.1.call-done = f32[256,128]{1,0:T(8,128)} async-done(((f32[2048,128]{1,0:T(8,128)}), f32[256,128]{1,0:T(8,128)}) %reduce-scatter.3.cloned.1.call-update) | async-done | bytes 131088 | tf_op jit(solution)/shard_map/reduce_scatter | solution.py:119
  530.3 36.3 %reduce-scatter.5.cloned.1.call-done = f32[256,128]{1,0:T(8,128)} async-done(((f32[2048,128]{1,0:T(8,128)}), f32[256,128]{1,0:T(8,128)}) %reduce-scatter.5.cloned.1.call-update) | async-done | bytes 131088 | tf_op jit(solution)/shard_map/reduce_scatter | solution.py:120
  (537 shorter events, 289.6 us)
Async XLA Ops:
  7.2 141.8 %all-gather.8.cloned.1.call-start = ((), (), s32[]{:S(2)}) async-start(), calls=%async_computation.5 | async-start | bytes 10813440 | tf_op jit(solution)/shard_map/all_gather | solution.py:13
  14.8 3.7 copy-start.5
  17.8 17.1 %copy-start.3 = (f32[10,2048]{1,0:T(8,128)S(1)}, f32[10,2048]{1,0:T(8,128)}, u32[]{:S(2)}) copy-start(f32[10,2048]{1,0:T(8,128)} %param.18) | copy-start | bytes 245764
  18.5 17.2 %copy-start = (f32[2048,640]{0,1:T(8,128)}, f32[2048,640]{0,1:T(8,128)S(1)}, u32[]{:S(2)}) copy-start(f32[2048,640]{0,1:T(8,128)S(1)} %convert_element_type.76) | copy-start | bytes 15728644
  39.0 3.8 copy-start.6
  39.0 226.0 %all-gather.6.cloned.1.call-start = ((), (), s32[]{:S(2)}) async-start(), calls=%async_computation.4 | async-start | bytes 10813440 | tf_op jit(solution)/shard_map/all_gather | solution.py:13
  42.1 14.0 %copy-start.4 = (f32[2048,10]{0,1:T(8,128)S(1)}, f32[2048,10]{0,1:T(8,128)}, u32[]{:S(2)}) copy-start(f32[2048,10]{0,1:T(8,128)} %get-tuple-element.1043) | copy-start | bytes 245764
  42.8 13.3 %copy-start.1 = (f32[2048,640]{0,1:T(8,128)}, f32[2048,640]{0,1:T(8,128)S(1)}, u32[]{:S(2)}) copy-start(f32[2048,640]{0,1:T(8,128)S(1)} %convert_element_type.74) | copy-start | bytes 15728644
  42.8 18.5 %copy-start.8 = (u32[256]{0:T(256)S(1)}, u32[256]{0:T(256)}, u32[]{:S(2)}) copy-start(u32[256]{0:T(256)} %constant.201) | copy-start | bytes 3076
  59.4 470.9 %reduce-scatter.3.cloned.1.call-start = ((), (), s32[]{:S(2)}) async-start(), calls=%async_computation.2 | async-start | bytes 1179648 | tf_op jit(solution)/shard_map/reduce_scatter | solution.py:119
  265.1 46.8 %copy-start.7 = (f32[10]{0:T(128)S(1)}, f32[10]{0:T(128)}, u32[]{:S(2)}) copy-start(f32[10]{0:T(128)} %param.19) | copy-start | bytes 124
  494.7 1.0 copy-start.2
  495.7 70.9 %reduce-scatter.5.cloned.1.call-start = ((), (), s32[]{:S(2)}) async-start(), calls=%async_computation.3 | async-start | bytes 1179648 | tf_op jit(solution)/shard_map/reduce_scatter | solution.py:120
Sparse Core Ops, SparseCore 0:
  39.1 109.8 all-gather.7
  151.6 106.1 all-gather.5
  495.9 34.3 reduce-scatter.2
  533.2 33.3 reduce-scatter.4
where the time goes:
time: 579 us; the launch traced here: 573 us
  matrix products  184 us (32%)
  local copies, waits for them, and re-layouts  124 us (21%)
  blocking collectives  93 us (16%)
  other arithmetic  78.9 us (14%)
  waiting for transfers between devices  68.7 us (12%)
  between operations  15.4 us (3%)
  loops' own time  8.71 us (2%)
    dot_general x16, matrix products, span_update(): jnp.einsum('hts,shp->thp', weights, feature_part, precision=lax.Precision...  68.6 us
    unnamed x1, blocking collectives  63.6 us
    dynamic_update_slice x32, other arithmetic, block_forward(): lax.scan(advance, state_in, (feature_blocks, write_blocks, read_blocks, l...  46 us
    dot_general x24, matrix products, span_update(): jnp.einsum('sn,shp->hnp', write_part, feature_part * tail_weight.T[:, :,...  39.5 us
    dynamic_slice x62, local copies, waits for them, and re-layouts, one(): lax.dynamic_index_in_dim(a, source, 0, False)  38.2 us
    dot_general x24, matrix products, span_update(): scores = jnp.dot(read_part, write_part.T, precision=lax.Precision.HIGHEST)  37.8 us
    reduce_scatter x1, waiting for transfers between devices, shards(): lax.psum_scatter(grad_read_all, 'head', scatter_dimension=0, tiled=True)  36.3 us
    dot_general x16, matrix products, span_update(): jnp.einsum('tn,hnp->thp', read_part, carry_state, precision=lax.Precision...  31.6 us
  transfers between devices with their start and end apart: 4, of which 3 were waited for; matrix products, arithmetic and copies ran while one was open for 25% of the time, Pallas kernels for 0%

commit v1 on v0

v1 whole, which is shorter than its diff:
```python
import functools

import jax
import jax.numpy as jnp
import numpy as np
from jax import lax
from jax.experimental import pallas as pl
from jax.experimental.pallas import tpu as pltpu
from jax.sharding import PartitionSpec as P

F32 = jnp.float32
BF16 = jnp.bfloat16
TOK = 2048
HEADS = 10
PAD = 16
WIDTH = 640
STATE = 128
Q = 128
CHUNKS = TOK // Q
BLOCK = 256
BLOCKS = TOK // BLOCK
VMEM = 28 * 1024 * 1024
LOG2E = 1.4426950408889634
NEG = -1e30


def spread(first):
    out = np.zeros((STATE, WIDTH), np.float32)
    for j in range(WIDTH):
        out[first + j // 64, j] = 1.0
        out[first + PAD + j // 64, j] = 1.0
    return out


SPREAD_D = np.concatenate([spread(0), spread(32)], axis=1)
SPREAD_C = np.concatenate([spread(64), spread(96)], axis=1)
SPREAD_F = spread(0)


def nt(a, b):
    return lax.dot_general(a, b, (((1,), (1,)), ((), ())), preferred_element_type=F32)


def tn(a, b):
    return lax.dot_general(a, b, (((0,), (0,)), ((), ())), preferred_element_type=F32)


def nn(a, b):
    return lax.dot_general(a, b, (((1,), (0,)), ((), ())), preferred_element_type=F32)


WHOLE = pl.BlockSpec(memory_space=pltpu.VMEM)
SCALARS = pl.BlockSpec(memory_space=pltpu.SMEM)
FAR = pl.BlockSpec(memory_space=pltpu.HBM)


def far(*arrays):
    return [pltpu.with_memory_space_constraint(a, pltpu.HBM) for a in arrays]


def far_out(shape, dtype):
    return pltpu.HBM(shape, dtype)


def block_copy(src, dst, sem, which, i, rows=BLOCK):
    r = pl.ds(pl.multiple_of(i * rows, rows), rows)
    return pltpu.make_async_copy(src.at[r], dst.at[r], sem.at[which, i])


def options():
    return pltpu.CompilerParams(vmem_limit_bytes=VMEM)


def cost(flops, moved):
    return pl.CostEstimate(flops=int(flops), bytes_accessed=int(moved), transcendentals=0)


def starts_until(off, t):
    count = jnp.where(t >= off[0, 0], 1, 0)
    for i in range(1, 4):
        count = count + jnp.where(t >= off[0, i], 1, 0)
    return count


def decay_part(off, l_ref, gain_ref, lg_ref, lrow_ref, lshift_ref, sc_ref, dec_ref):
    lane = lax.broadcasted_iota(jnp.int32, (PAD, Q), 1)
    rev = [None] * CHUNKS
    fwd = [None] * CHUNKS
    for c in range(CHUNKS):
        x = l_ref[:, c * Q : (c + 1) * Q]
        y, z = x, x
        for k in (1, 2, 4, 8, 16, 32, 64):
            y = y + jnp.where(lane >= k, pltpu.roll(y, k, 1), 0.0)
            z = z + jnp.where(lane < Q - k, pltpu.roll(z, Q - k, 1), 0.0)
        fwd[c] = y
        rev[c] = jnp.where(lane < Q - 1, pltpu.roll(z, Q - 1, 1), 0.0)
    ends = [fwd[c][:, Q - 1 : Q] for c in range(CHUNKS)]
    before = [jnp.zeros((PAD, 1), F32)]
    for c in range(CHUNKS):
        before.append(before[-1] + ends[c])
    after = [jnp.zeros((PAD, 1), F32)]
    for c in range(CHUNKS - 1, 0, -1):
        after.append(after[-1] + ends[c])
    after = after[::-1]
    last_count = starts_until(off, jnp.int32(TOK - 1))
    decs = jnp.zeros((PAD, Q), F32)
    for c in range(CHUNKS):
        t = lane + c * Q
        seg = starts_until(off, t)
        seg_b = starts_until(off, jnp.int32(c * Q - 1))
        seg_e = starts_until(off, jnp.int32(c * Q + Q - 1))
        gain = gain_ref[:, c * Q : (c + 1) * Q]
        tail_d = jnp.where(seg == last_count, jnp.exp2(rev[c] + after[c]) * gain, 0.0)
        entry_d = jnp.where(seg == 0, jnp.exp2(fwd[c] + before[c]), 0.0)
        tail_c = jnp.where(seg == seg_e, jnp.exp2(rev[c]) * gain, 0.0)
        entry_c = jnp.where(seg == seg_b, jnp.exp2(fwd[c]), 0.0)
        rows = []
        for v in (tail_d, entry_d, tail_c, entry_c):
            hi = v.astype(BF16).astype(F32)
            rows += [hi, v - hi]
        sc_ref[c * Q : (c + 1) * Q, :] = jnp.concatenate(rows, axis=0).T.astype(BF16)
        lrow_ref[:, c * Q : (c + 1) * Q] = fwd[c]
        lshift_ref[:, c * Q : (c + 1) * Q] = fwd[c] - lg_ref[:, c * Q : (c + 1) * Q]
        keep_c = jnp.where(seg_b == seg_e, 1.0, 0.0)
        decs = jnp.where(lane == c, jnp.exp2(ends[c]) * keep_c, decs)
        keep_after = jnp.where(seg_e == last_count, 1.0, 0.0)
        decs = jnp.where(lane == 32 + c, jnp.exp2(after[c]) * keep_after, decs)
    keep = jnp.where(last_count == 0, 1.0, 0.0)
    decs = jnp.where(lane == CHUNKS, jnp.exp2(before[CHUNKS]) * keep, decs)
    hi = decs.astype(BF16).astype(F32)
    full = jnp.concatenate([hi, decs - hi, jnp.zeros((Q - 2 * PAD, Q), F32)], axis=0)
    dec_ref[...] = full.T.astype(BF16)


def prepare_kernel(
    off, l_ref, gain_ref, lg_ref, x_hbm, g_hbm, sp_ref,
    lrow_ref, lshift_ref, sc_ref, dec_ref, xt_hbm, ge_hbm, x_ref, g_ref, in_sem, out_sem,
):
    for i in range(BLOCKS):
        block_copy(x_hbm, x_ref, in_sem, 0, i).start()
        block_copy(g_hbm, g_ref, in_sem, 1, i).start()
    decay_part(off, l_ref, gain_ref, lg_ref, lrow_ref, lshift_ref, sc_ref, dec_ref)

    @pl.loop(0, BLOCKS)
    def _(i):
        block_copy(x_hbm, x_ref, in_sem, 0, i).wait()
        block_copy(g_hbm, g_ref, in_sem, 1, i).wait()
        r = pl.ds(pl.multiple_of(i * BLOCK, BLOCK), BLOCK)
        s = nn(sc_ref[r, :], sp_ref[...])
        x_ref[r, :] = (x_ref[r, :].astype(F32) * s[:, :WIDTH]).astype(BF16)
        g_ref[r, :] = (g_ref[r, :].astype(F32) * s[:, WIDTH:]).astype(BF16)
        block_copy(x_ref, xt_hbm, out_sem, 0, i).start()
        block_copy(g_ref, ge_hbm, out_sem, 1, i).start()

    for i in range(BLOCKS):
        block_copy(x_ref, xt_hbm, out_sem, 0, i).wait()
        block_copy(g_ref, ge_hbm, out_sem, 1, i).wait()


def prepare_call(off, log_decay, x, g, sp):
    l = jnp.pad(log_decay, ((0, PAD - HEADS), (0, 0)), constant_values=-1.0)
    square = -jnp.expm1(2.0 * l)
    return pl.pallas_call(
        prepare_kernel,
        out_shape=(
            jax.ShapeDtypeStruct((PAD, TOK), F32),
            jax.ShapeDtypeStruct((PAD, TOK), F32),
            far_out((TOK, STATE), BF16),
            jax.ShapeDtypeStruct((STATE, STATE), BF16),
            far_out((TOK, WIDTH), BF16),
            far_out((TOK, WIDTH), BF16),
        ),
        in_specs=[SCALARS, WHOLE, WHOLE, WHOLE, FAR, FAR, WHOLE],
        out_specs=(WHOLE,) * 4 + (FAR,) * 2,
        scratch_shapes=[pltpu.VMEM((TOK, WIDTH), BF16)] * 2 + [pltpu.SemaphoreType.DMA((2, BLOCKS))] * 2,
        compiler_params=options(),
        cost_estimate=cost(4e9, 16e6),
        name="prepare",
    )(off, l * LOG2E, jnp.sqrt(square), 0.5 * jnp.log2(square), *far(x, g), sp)


def state_kernel(
    place, m0, m1, m2, m3, o0, o1, o2, o3, xt_hbm, ge_hbm, dec_ref, out_ref, bc_hbm,
    xt_ref, ge_ref, bc_ref, in_sem, out_sem,
):
    rows = TOK // 4
    for i in range(4):
        block_copy(xt_hbm, xt_ref, in_sem, 0, i, rows).start()
        block_copy(ge_hbm, ge_ref, in_sem, 1, i, rows).start()
    core, y = place[0], place[1]
    for k, (m, o) in enumerate(((m0, o0), (m1, o1), (m2, o2), (m3, o3))):
        pair = lax.rem(y + 4 - k, 4) * 2
        bc_ref[pl.ds(pl.multiple_of((pair + core) * BLOCK, BLOCK), BLOCK), :] = m[...]
        bc_ref[pl.ds(pl.multiple_of((pair + 1 - core) * BLOCK, BLOCK), BLOCK), :] = o[...]
    save = pltpu.make_async_copy(bc_ref, bc_hbm, out_sem)
    save.start()
    for i in range(4):
        block_copy(xt_hbm, xt_ref, in_sem, 0, i, rows).wait()
        block_copy(ge_hbm, ge_ref, in_sem, 1, i, rows).wait()
    s = nn(bc_ref[:, :STATE].T, xt_ref[...])
    out_ref[:16, :, :WIDTH] = s.reshape(16, 8, WIDTH).astype(BF16)
    t = nn(bc_ref[:, STATE:].T, ge_ref[...])
    out_ref[16:, :, :WIDTH] = t.reshape(16, 8, WIDTH).astype(BF16)
    row = dec_ref[CHUNKS : CHUNKS + 1, :].astype(F32)
    out_ref[:, :, WIDTH:] = jnp.broadcast_to(row[None], (32, 8, STATE)).astype(BF16)
    save.wait()


def state_call(place, pieces, xt, ge, dec):
    return pl.pallas_call(
        state_kernel,
        out_shape=(jax.ShapeDtypeStruct((32, 8, WIDTH + STATE), BF16), far_out((TOK, 2 * STATE), BF16)),
        in_specs=[SCALARS] + [WHOLE] * 8 + [FAR, FAR, WHOLE],
        out_specs=(WHOLE, FAR),
        scratch_shapes=[pltpu.VMEM((TOK, WIDTH), BF16)] * 2
        + [pltpu.VMEM((TOK, 2 * STATE), BF16), pltpu.SemaphoreType.DMA((2, 4)), pltpu.SemaphoreType.DMA],
        compiler_params=options(),
        cost_estimate=cost(7e8, 6.5e6),
        name="states",
    )(place, *pieces, *far(xt, ge), dec)


def scan_kernel(me, in_ref, sp_ref, out_ref, d_ref):
    rows = in_ref[:, :, WIDTH:].astype(F32).reshape(256, STATE).astype(BF16)
    d_ref[...] = nn(rows, sp_ref[...]).reshape(32, 8, WIDTH)
    backward = me[0] >= 16

    def one(k, state):
        b = jnp.where(backward, 31 - k, k)
        out_ref[b] = state.astype(BF16)
        return d_ref[b] * state + in_ref[b, :, :WIDTH].astype(F32)

    lax.fori_loop(0, 32, one, jnp.zeros((8, WIDTH), F32), unroll=True)


def scan_call(me, part, sp):
    vm = pl.BlockSpec(memory_space=pltpu.VMEM)
    return pl.pallas_call(
        scan_kernel,
        out_shape=jax.ShapeDtypeStruct((32, 8, WIDTH), BF16),
        in_specs=[pl.BlockSpec(memory_space=pltpu.SMEM), vm, vm],
        out_specs=vm,
        scratch_shapes=[pltpu.VMEM((32, 8, WIDTH), F32)],
        compiler_params=pltpu.CompilerParams(vmem_limit_bytes=VMEM),
        name="scan",
    )(me, part, sp)


def within_kernel(
    off, x_hbm, g_hbm, bc_hbm, lrow_ref, lshift_ref, skip_ref, gx_hbm, z_hbm,
    x_ref, g_ref, bc_ref, gx_ref, z_ref, in_sem, out_sem,
):
    for i in range(BLOCKS):
        block_copy(bc_hbm, bc_ref, in_sem, 2, i).start()
        block_copy(x_hbm, x_ref, in_sem, 0, i).start()
        block_copy(g_hbm, g_ref, in_sem, 1, i).start()
    si = lax.broadcasted_iota(jnp.int32, (Q, Q), 0)
    ti = lax.broadcasted_iota(jnp.int32, (Q, Q), 1)
    even = lax.broadcasted_iota(jnp.int32, (Q, Q), 1) < 64
    odd = jnp.logical_not(even)
    zero = jnp.zeros((Q, Q), BF16)

    @pl.loop(0, BLOCKS)
    def _(step):
        block_copy(bc_hbm, bc_ref, in_sem, 2, step).wait()
        block_copy(x_hbm, x_ref, in_sem, 0, step).wait()
        block_copy(g_hbm, g_ref, in_sem, 1, step).wait()
        for sub in range(BLOCK // Q):
            base = pl.multiple_of(step * BLOCK + sub * Q, Q)
            r = pl.ds(base, Q)
            same = starts_until(off, si + base) == starts_until(off, ti + base)
            bias = jnp.where((ti >= si) & same, 0.0, NEG)
            lt = lrow_ref[:, r]
            ls = lshift_ref[:, r].T
            scores = nt(bc_ref[r, :STATE], bc_ref[r, STATE:])
            z = jnp.zeros((Q, Q), F32)
            for p in range(HEADS // 2):
                w = slice(p * Q, (p + 1) * Q)
                x = x_ref[r, w]
                g = g_ref[r, w]
                e = nt(jnp.concatenate([jnp.where(even, x, zero), jnp.where(odd, x, zero)], axis=0), g)
                h = 2 * p
                ma = jnp.exp2(lt[h : h + 1, :] - ls[:, h : h + 1] + bias)
                mb = jnp.exp2(lt[h + 1 : h + 2, :] - ls[:, h + 1 : h + 2] + bias)
                z = z + (ma * e[:Q] + mb * e[Q:])
                weights = jnp.concatenate([(ma * scores).astype(BF16), (mb * scores).astype(BF16)], axis=1)
                both = jnp.concatenate([jnp.where(even, g, zero), jnp.where(odd, g, zero)], axis=0)
                gx_ref[r, w] = (nn(weights, both) + g.astype(F32) * skip_ref[:, w]).astype(BF16)
            z_ref[r, :] = z.astype(BF16)
        block_copy(gx_ref, gx_hbm, out_sem, 0, step).start()
        block_copy(z_ref, z_hbm, out_sem, 1, step).start()

    for i in range(BLOCKS):
        block_copy(gx_ref, gx_hbm, out_sem, 0, i).wait()
        block_copy(z_ref, z_hbm, out_sem, 1, i).wait()


def within_call(off, x, g, bc, lrow, lshift, skip):
    return pl.pallas_call(
        within_kernel,
        out_shape=(far_out((TOK, WIDTH), BF16), far_out((TOK, STATE), BF16)),
        in_specs=[SCALARS, FAR, FAR, FAR, WHOLE, WHOLE, WHOLE],
        out_specs=(FAR, FAR),
        scratch_shapes=[
            pltpu.VMEM((TOK, WIDTH), BF16),
            pltpu.VMEM((TOK, WIDTH), BF16),
            pltpu.VMEM((TOK, 2 * STATE), BF16),
            pltpu.VMEM((TOK, WIDTH), BF16),
            pltpu.VMEM((TOK, STATE), BF16),
            pltpu.SemaphoreType.DMA((3, BLOCKS)),
            pltpu.SemaphoreType.DMA((2, BLOCKS)),
        ],
        compiler_params=options(),
        cost_estimate=cost(4e9, 16e6),
        name="within_chunks",
    )(off, *far(x, g, bc), lrow, lshift, skip)


def chain_kernel(
    x_hbm, g_hbm, bc_hbm, sc_hbm, z_hbm, dec_ref, sp_ref, spf_ref, gc_hbm, gb_hbm, tst_hbm,
    x_ref, g_ref, bc_ref, sc_ref, z_ref, gc_ref, gb_ref, tst_ref, s_ref, t_ref, d_ref, in_sem, out_sem,
):
    loads = ((sc_hbm, sc_ref), (x_hbm, x_ref), (g_hbm, g_ref), (bc_hbm, bc_ref), (z_hbm, z_ref))
    for i in range(BLOCKS // 2):
        for j in (i, BLOCKS - 1 - i):
            for n, (src, dst) in enumerate(loads):
                block_copy(src, dst, in_sem, n, j).start()
    s_ref[...] = jnp.zeros_like(s_ref)
    t_ref[...] = jnp.zeros_like(t_ref)
    d_ref[...] = nn(dec_ref[:CHUNKS, :], spf_ref[...])
    per = BLOCK // Q

    @pl.loop(0, BLOCKS)
    def _(step):
        @pl.when(step < BLOCKS // 2)
        def _():
            for j in (step, BLOCKS - 1 - step):
                for n, (src, dst) in enumerate(loads):
                    block_copy(src, dst, in_sem, n, j).wait()
                for sub in range(per):
                    r = pl.ds(pl.multiple_of(j * BLOCK + sub * Q, Q), Q)
                    s = nn(sc_ref[r, :], sp_ref[...])
                    x_ref[r, :] = (x_ref[r, :].astype(F32) * s[:, :WIDTH]).astype(BF16)
                    g_ref[r, :] = (g_ref[r, :].astype(F32) * s[:, WIDTH:]).astype(BF16)

        back = BLOCKS - 1 - step
        for sub in range(per):
            c = step * per + sub
            r = pl.ds(pl.multiple_of(c * Q, Q), Q)
            state = s_ref[...]
            b = bc_ref[r, :STATE]
            gc_ref[r, :] = tn(z_ref[r, :], b) + nt(g_ref[r, :], state.astype(BF16))
            s_ref[...] = d_ref[pl.ds(c, 1), :] * state + tn(b, x_ref[r, :])
            c = back * per + per - 1 - sub
            r = pl.ds(pl.multiple_of(c * Q, Q), Q)
            state = t_ref[...]
            low = state.astype(BF16)
            tst_ref[c] = low
            q = bc_ref[r, STATE:]
            gb_ref[r, :] = nn(z_ref[r, :], q) + nt(x_ref[r, :], low)
            t_ref[...] = d_ref[pl.ds(c, 1), :] * state + tn(q, g_ref[r, :])
        block_copy(gc_ref, gc_hbm, out_sem, 0, step).start()
        block_copy(gb_ref, gb_hbm, out_sem, 1, back).start()
        block_copy(tst_ref, tst_hbm, out_sem, 2, back, per).start()

    for i in range(BLOCKS):
        block_copy(gc_ref, gc_hbm, out_sem, 0, i).wait()
        block_copy(gb_ref, gb_hbm, out_sem, 1, i).wait()
        block_copy(tst_ref, tst_hbm, out_sem, 2, i, per).wait()


def chain_call(x, g, bc, sc, z, dec, sp, spf):
    return pl.pallas_call(
        chain_kernel,
        out_shape=(
            far_out((TOK, STATE), F32),
            far_out((TOK, STATE), F32),
            far_out((CHUNKS, STATE, WIDTH), BF16),
        ),
        in_specs=[FAR] * 5 + [WHOLE] * 3,
        out_specs=(FAR,) * 3,
        scratch_shapes=[
            pltpu.VMEM((TOK, WIDTH), BF16),
            pltpu.VMEM((TOK, WIDTH), BF16),
            pltpu.VMEM((TOK, 2 * STATE), BF16),
            pltpu.VMEM((TOK, STATE), BF16),
            pltpu.VMEM((TOK, STATE), BF16),
            pltpu.VMEM((TOK, STATE), F32),
            pltpu.VMEM((TOK, STATE), F32),
            pltpu.VMEM((CHUNKS, STATE, WIDTH), BF16),
            pltpu.VMEM((STATE, WIDTH), F32),
            pltpu.VMEM((STATE, WIDTH), F32),
            pltpu.VMEM((CHUNKS, WIDTH), F32),
            pltpu.SemaphoreType.DMA((5, BLOCKS)),
            pltpu.SemaphoreType.DMA((3, BLOCKS)),
        ],
        compiler_params=options(),
        cost_estimate=cost(4e9, 16e6),
        name="chunk_chain",
    )(*far(x, g, bc, sc, z), dec, sp, spf)


def carry_kernel(
    place, xt_hbm, ge_hbm, gb_hbm, gc_hbm, st_ref, keep_ref, send_ref, xt_ref, ge_ref, gb_ref, gc_ref, in_sem
):
    core = place[0]
    loads = ((xt_hbm, xt_ref), (ge_hbm, ge_ref), (gb_hbm, gb_ref), (gc_hbm, gc_ref))
    for i in range(BLOCKS):
        for n, (src, dst) in enumerate(loads):
            block_copy(src, dst, in_sem, n, i).start()
    s = st_ref[:STATE, :]
    t = st_ref[STATE:, :]
    for i in range(4):
        for n, (src, dst) in enumerate(loads):
            block_copy(src, dst, in_sem, n, 2 * i).wait()
            block_copy(src, dst, in_sem, n, 2 * i + 1).wait()
        r = pl.ds(pl.multiple_of((2 * i + core) * BLOCK, BLOCK), BLOCK)
        keep_ref[i, :, :STATE] = gb_ref[r, :] + nt(xt_ref[r, :], t)
        keep_ref[i, :, STATE:] = gc_ref[r, :] + nt(ge_ref[r, :], s)
        r = pl.ds(pl.multiple_of((2 * i + 1 - core) * BLOCK, BLOCK), BLOCK)
        send_ref[i, :, :STATE] = (gb_ref[r, :] + nt(xt_ref[r, :], t)).astype(BF16)
        send_ref[i, :, STATE:] = (gc_ref[r, :] + nt(ge_ref[r, :], s)).astype(BF16)


def carry_call(place, xt, ge, gb, gc, st):
    return pl.pallas_call(
        carry_kernel,
        out_shape=(
            jax.ShapeDtypeStruct((4, BLOCK, 2 * STATE), F32),
            jax.ShapeDtypeStruct((4, BLOCK, 2 * STATE), BF16),
        ),
        in_specs=[SCALARS] + [FAR] * 4 + [WHOLE],
        out_specs=(WHOLE, WHOLE),
        scratch_shapes=[
            pltpu.VMEM((TOK, WIDTH), BF16),
            pltpu.VMEM((TOK, WIDTH), BF16),
            pltpu.VMEM((TOK, STATE), F32),
            pltpu.VMEM((TOK, STATE), F32),
            pltpu.SemaphoreType.DMA((4, BLOCKS)),
        ],
        compiler_params=options(),
        cost_estimate=cost(7e8, 9e6),
        name="carry",
    )(place, *far(xt, ge, gb, gc), st)


def input_kernel(
    gx_hbm, tst_hbm, bc_hbm, sc_hbm, st_ref, sp_ref, dec_ref, spf_ref, out_hbm,
    gx_ref, tst_ref, bc_ref, sc_ref, d_ref, in_sem, out_sem,
):
    per = BLOCK // Q
    loads = ((gx_hbm, gx_ref, BLOCK), (tst_hbm, tst_ref, per), (bc_hbm, bc_ref, BLOCK), (sc_hbm, sc_ref, BLOCK))
    for i in range(BLOCKS):
        for n, (src, dst, rows) in enumerate(loads):
            block_copy(src, dst, in_sem, n, i, rows).start()
    d_ref[...] = nn(dec_ref[32 : 32 + CHUNKS, :], spf_ref[...])

    @pl.loop(0, BLOCKS)
    def _(step):
        for n, (src, dst, rows) in enumerate(loads):
            block_copy(src, dst, in_sem, n, step, rows).wait()
        for sub in range(per):
            c = step * per + sub
            r = pl.ds(pl.multiple_of(c * Q, Q), Q)
            full = tst_ref[c].astype(F32) + d_ref[pl.ds(c, 1), :] * st_ref[STATE:, :].astype(F32)
            scale = nn(sc_ref[r, :], sp_ref[:, :WIDTH])
            gx_ref[r, :] = (gx_ref[r, :].astype(F32) + scale * nn(bc_ref[r, :STATE], full.astype(BF16))).astype(BF16)
        block_copy(gx_ref, out_hbm, out_sem, 0, step).start()

    for i in range(BLOCKS):
        block_copy(gx_ref, out_hbm, out_sem, 0, i).wait()


def input_call(gx, tst, st, bc, sc, sp, dec, spf):
    return pl.pallas_call(
        input_kernel,
        out_shape=jax.ShapeDtypeStruct((TOK, WIDTH), BF16),
        in_specs=[FAR] * 4 + [WHOLE] * 4,
        out_specs=FAR,
        scratch_shapes=[
            pltpu.VMEM((TOK, WIDTH), BF16),
            pltpu.VMEM((CHUNKS, STATE, WIDTH), BF16),
            pltpu.VMEM((TOK, 2 * STATE), BF16),
            pltpu.VMEM((TOK, STATE), BF16),
            pltpu.VMEM((CHUNKS, WIDTH), F32),
            pltpu.SemaphoreType.DMA((4, BLOCKS)),
            pltpu.SemaphoreType.DMA((1, BLOCKS)),
        ],
        compiler_params=options(),
        cost_estimate=cost(2e9, 12e6),
        name="input_gradient",
    )(*far(gx, tst, bc, sc), st, sp, dec, spf)


def join_kernel(a_ref, b_ref, out_ref):
    out_ref[:, :STATE] = a_ref[...]
    out_ref[:, STATE:] = b_ref[...]


def join_call(a, b):
    return pl.pallas_call(
        join_kernel, out_shape=jax.ShapeDtypeStruct((BLOCK, 2 * STATE), BF16), compiler_params=options(), name="join"
    )(a, b)


def pair_kernel(place, keep_ref, got_ref, o0, o1, o2, o3):
    y = place[1]
    for k, o in enumerate((o0, o1, o2, o3)):
        j = lax.rem(y + k, 4)
        o[...] = (keep_ref[j] + got_ref[j].astype(F32)).astype(o.dtype)


def pair_call(place, keep, got):
    return pl.pallas_call(
        pair_kernel,
        out_shape=(jax.ShapeDtypeStruct((BLOCK, 2 * STATE), F32),)
        + (jax.ShapeDtypeStruct((BLOCK, 2 * STATE), BF16),) * 3,
        in_specs=[SCALARS, WHOLE, WHOLE],
        out_specs=(WHOLE,) * 4,
        compiler_params=options(),
        name="pair_sums",
    )(place, keep, got)


def total_kernel(a_ref, b_ref, c_ref, d_ref, w_ref, r_ref):
    t = a_ref[...] + b_ref[...].astype(F32) + c_ref[...].astype(F32) + d_ref[...].astype(F32)
    w_ref[...] = t[:, :STATE]
    r_ref[...] = t[:, STATE:]


def total_call(*parts):
    return pl.pallas_call(
        total_kernel,
        out_shape=(jax.ShapeDtypeStruct((BLOCK, STATE), F32),) * 2,
        compiler_params=options(),
        name="totals",
    )(*parts)


def along_y(k):
    return [(i, (i + 2 * k) % 8) for i in range(8)]


SWAP = [(i, i ^ 1) for i in range(8)]


def shards(mixer_input, write_rows, read_rows, log_decay, skip_gain, reset_offsets, grad_out):
    spot = lax.axis_index("head").astype(jnp.int32)
    core, y = spot & 1, spot >> 1
    place = jnp.stack([core, y])
    me = lax.axis_index("seq").astype(jnp.int32).reshape(1)
    spread_d, spread_c, spread_f = (jnp.asarray(a, BF16) for a in (SPREAD_D, SPREAD_C, SPREAD_F))
    own = join_call(write_rows, read_rows)
    mine = [own] + [lax.ppermute(own, "head", along_y(k)) for k in (1, 2, 3)]
    lrow, lshift, sc, dec, xt, ge = prepare_call(reset_offsets, log_decay, mixer_input, grad_out, spread_d)
    *mine, xt, ge = lax.optimization_barrier((*mine, xt, ge))
    other = [lax.ppermute(a, "head", SWAP) for a in mine]
    payload, bc = state_call(place, mine + other, xt, ge, dec)
    parts = lax.all_to_all(payload, "seq", 0, 0, tiled=True)
    skip = jnp.repeat(skip_gain, 64)[None, :]
    gx, z = within_call(reset_offsets, mixer_input, grad_out, bc, lrow, lshift, skip)
    parts, gx, z = lax.optimization_barrier((parts, gx, z))
    entering = scan_call(me, parts, spread_f)
    st = lax.all_to_all(entering, "seq", 0, 0, tiled=True).reshape(2 * STATE, WIDTH)
    gc, gb, tst = chain_call(mixer_input, grad_out, bc, sc, z, dec, spread_c, spread_f)
    keep, send = carry_call(place, xt, ge, gb, gc, st)
    total, *leaving = pair_call(place, keep, lax.ppermute(send, "head", SWAP))
    arrived = [lax.ppermute(a, "head", along_y(k)) for k, a in zip((1, 2, 3), leaving)]
    grad_input = input_call(gx, tst, st, bc, sc, spread_c, dec, spread_f)
    return (grad_input, *total_call(total, *arrived))


def solution(mesh):
    in_specs = (
        P("seq", "head"),
        P(("seq", "head"), None),
        P(("seq", "head"), None),
        P("head", "seq"),
        P("head"),
        P("seq", None),
        P("seq", "head"),
    )
    out_specs = (P("seq", "head"), P(("seq", "head"), None), P(("seq", "head"), None))
    return jax.shard_map(shards, mesh=mesh, in_specs=in_specs, out_specs=out_specs, check_vma=False)
```

time: 579 us -> 90.6 us (0.16)
  matrix products: 184 us -> 0 us
  local copies, waits for them, and re-layouts: 124 us -> 3.46 us
  blocking collectives: 93 us -> 0 us
  other arithmetic: 78.9 us -> 1.08 us
  waiting for transfers between devices: 68.7 us -> 9.65 us
  Pallas kernels: 0 us -> 45.5 us
  starting transfers between devices: 0.43 us -> 29.7 us
  between operations: 15.4 us -> 0.8 us
  loops' own time: 8.71 us -> 0 us
    dot_general x82 -> x0, matrix products: 184 us -> none  [the longest x16 68.6 us: span_update(): jnp.einsum('hts,shp->thp', weights, feature_part, precision=lax.Precision...]
    unnamed x1 -> x0, blocking collectives: 63.6 us -> none
    reduce_scatter x2 -> x0, waiting for transfers between devices: 63.4 us -> none  [the longest x1 36.3 us: shards(): lax.psum_scatter(grad_read_all, 'head', scatter_dimension=0, tiled=True)]
    dynamic_slice x86 -> x0, local copies, waits for them, and re-layouts: 62.7 us -> none  [the longest x62 38.2 us: one(): lax.dynamic_index_in_dim(a, source, 0, False)]
    dynamic_update_slice x32 -> x0, other arithmetic: 46 us -> none  [block_forward(): lax.scan(advance, state_in, (feature_blocks, write_blocks, read_blocks, l...]
    pallas_call x0 -> x10, Pallas kernels: none -> 45.5 us  [the longest x1 9.98 us: within_call(): pl.pallas_call(within_kernel, out_shape=(far_out((TOK, WIDTH), BF16), far...]
    all_gather x2 -> x0, blocking collectives: 29.4 us -> none  [the longest x1 16.2 us: shards(): lax.all_gather(write_rows, 'head', axis=0, tiled=True)]
    unnamed x33 -> x16, local copies, waits for them, and re-layouts: 28.9 us -> 3.31 us
  transfers between devices with their start and end apart: 4 -> 13, of which waited for: 3 -> 8; matrix products, arithmetic and copies ran while one was open for 25% -> 1% of each run, Pallas kernels for 0% -> 37%
where the time goes in v1:
time: 90.6 us; the launch traced here: 90.1 us
  Pallas kernels  45.5 us (50%)
  starting transfers between devices  29.7 us (33%)
  waiting for transfers between devices  9.65 us (11%)
  local copies, waits for them, and re-layouts  3.46 us (4%)
  other arithmetic  1.08 us (1%)
    all_to_all x1, starting transfers between devices, shards(): parts = lax.all_to_all(payload, 'seq', 0, 0, tiled=True)  11.1 us
    pallas_call x1, Pallas kernels, within_call(): pl.pallas_call(within_kernel, out_shape=(far_out((TOK, WIDTH), BF16), far...  9.98 us
    pallas_call x1, Pallas kernels, chain_call(): pl.pallas_call(chain_kernel, out_shape=(far_out((TOK, STATE), F32), far_o...  9.85 us
    pallas_call x1, Pallas kernels, prepare_call(): pl.pallas_call(prepare_kernel, out_shape=(jax.ShapeDtypeStruct((PAD, TOK)...  8.59 us
    pallas_call x1, Pallas kernels, state_call(): pl.pallas_call(state_kernel, out_shape=(jax.ShapeDtypeStruct((32, 8, WIDT...  5.24 us
    all_to_all x1, starting transfers between devices, shards(): lax.all_to_all(entering, 'seq', 0, 0, tiled=True).reshape(2 * STATE, WIDTH)  5.18 us
    pallas_call x1, Pallas kernels, input_call(): pl.pallas_call(input_kernel, out_shape=jax.ShapeDtypeStruct((TOK, WIDTH),...  4.9 us
    ppermute x3, starting transfers between devices, shards(): mine = [own] + [lax.ppermute(own, 'head', along_y(k)) for k in (1, 2, 3)]  4.68 us
  transfers between devices with their start and end apart: 13, of which 8 were waited for; matrix products, arithmetic and copies ran while one was open for 1% of the time, Pallas kernels for 37%

profile of v1, /device:TPU:1, one launch (start us, length us, event | category | flops | bytes accessed | tf_op | source)
XLA Modules:
  0.0 90.1 jit_solution(15495737396245600141)
XLA Ops:
  0.6 0.8 copy-done.2
  1.5 0.8 copy-done.3
  2.3 3.6 %collective-permute-start.2 = (bf16[256,256]{1,0:T(8,128)(2,1)S(1)}, bf16[256,256]{1,0:T(8,128)(2,1)S(1)}, u32[]{:S(2)}, u32[]{:S(2)}) collective-permute-start(bf16[256,256]{1,0:T(8,128)(2,1)S(1)} %join.1.m0), channel_id=1, source_target_pairs={{0,6},{1,7},{2,0},{3,1},{4,2},{5,3},{6,4},{7,5},{8,14},{9,15},{10,... | collective-permute-start | bytes 393224 | tf_op jit(solution)/shard_map/ppermute | solution.py:554
  6.0 0.3 collective-permute-start.1
  6.3 0.7 collective-permute-start
  7.0 1.0 %log_multiply_fusion = (f32[16,2048]{1,0:T(8,128)S(1)}, f32[16,2048]{1,0:T(8,128)S(1)}, f32[16,2048]{1,0:T(8,128)S(1)}) fusion(f32[10,2048]{1,0:T(8,128)} %param.13), kind=kLoop, calls=%fused_computation | loop fusion | flops 131072 | bytes 475136 | tf_op jit(solution)/shard_map/mul | solution.py:179
  8.0 0.6 copy-done.4
  8.7 1.0 %copy-done.6 = bf16[128,1280]{1,0:T(8,128)(2,1)S(1)} copy-done((bf16[128,1280]{1,0:T(8,128)(2,1)S(1)}, bf16[128,1280]{1,0:T(8,128)(2,1)}, u32[]{:S(2)}) %copy-start.6) | copy-done | bytes 327704
  9.7 8.6 %prepare.1 = (f32[16,2048]{1,0:T(8,128)S(1)}, f32[16,2048]{1,0:T(8,128)S(1)}, bf16[2048,128]{1,0:T(8,128)(2,1)}, bf16[128,128]{1,0:T(8,128)(2,1)S(1)}, bf16[2048...) custom-call(s32[1,4]{1,0:T(1,128)S(1)} %copy-done.4, f32[16,2048]{1,0:T(8,128)S(1)} %get-tuple-element.65.l_ref, ...), custom_call_target="tpu_custom_call" | custom-call | flops 4000000000 | bytes 16000000 | tf_op jit(solution)/shard_map/prepare/pallas_call | solution.py:163
  18.3 1.6 %collective-permute-start.3 = (bf16[256,256]{1,0:T(8,128)(2,1)S(1)}, bf16[256,256]{1,0:T(8,128)(2,1)S(1)}, u32[]{:S(2)}, u32[]{:S(2)}) collective-permute-start(bf16[256,256]{1,0:T(8,128)(2,1)S(1)} %join.1.m0), channel_id=1, source_target_pairs={{0,1},{1,0},{2,3},{3,2},{4,5},{5,4},{6,7},{7,6},{8,9},{9,8},{10,11... | collective-permute-start | bytes 393224 | tf_op jit(solution)/shard_map/ppermute | solution.py:557
  20.0 0.4 collective-permute-start.5
  20.6 0.3 collective-permute-done.3.o0
  20.9 0.4 collective-permute-done.4.o1
  21.4 0.3 collective-permute-done.6.o3
  21.8 5.2 %states.1 = (bf16[32,8,768]{2,1,0:T(8,128)(2,1)}, bf16[2048,256]{1,0:T(8,128)(2,1)}) custom-call(s32[2]{0:T(128)S(1)} %pad_add_fusion.place, bf16[256,256]{1,0:T(8,128)(2,1)S(1)} %join.1.m0, bf16[256,256]{1,0:T(8,128)(2,1)S(1)} %collective-permute-done.m1, bf16[256,256]{1,0:T(8,128)(2,1)S(1)} %collective-permute-done.1.m2, ...), custom_call_target="tpu_custom_call" | custom-call | flops 700000000 | bytes 6500000 | tf_op jit(solution)/shard_map/states/pallas_call | solution.py:210
  27.0 11.1 %all-to-all-start = ((bf16[32,8,768]{2,1,0:T(8,128)(2,1)}), bf16[32,8,768]{2,1,0:T(8,128)(2,1)S(1)}, u32[]{:S(2)}, u32[]{:S(2)}) async-start(bf16[32,8,768]{2,1,0:T(8,128)(2,1)} %get-tuple-element.42), calls=%async_computation | async-start | bytes 786432 | tf_op jit(solution)/shard_map/all_to_all | solution.py:559
  38.2 10.0 %within_chunks.1 = (bf16[2048,640]{1,0:T(8,128)(2,1)}, bf16[2048,128]{1,0:T(8,128)(2,1)}) custom-call(s32[1,4]{1,0:T(1,128)S(1)} %copy-done.5, bf16[2048,640]{1,0:T(8,128)(2,1)} %x_hbm.5, bf16[2048,640]{1,0:T(8,128)(2,1)} %g_hbm.5, bf16[2048,256]{1,0:T(8,128)(2,1)} %get-tuple-element.43.bc_hbm, f32[16,2048]{1,0:T(8,128)S(1)} %get-tuple-element.44.lrow_ref, ...), custom_call_target="tpu_custom_call" | custom-call | flops 4000000000 | bytes 16000000 | tf_op jit(solution)/shard_map/within_chunks/pallas_call | solution.py:299
  48.2 4.2 %all-to-all-done.in_ref = bf16[32,8,768]{2,1,0:T(8,128)(2,1)S(1)} async-done(((bf16[32,8,768]{2,1,0:T(8,128)(2,1)}), bf16[32,8,768]{2,1,0:T(8,128)(2,1)S(1)}, u32[]{:S(2)}, u32[]{:S(2)}) %all-to-all-start) | async-done | bytes 393248 | tf_op jit(solution)/shard_map/all_to_all | solution.py:559
  52.5 1.1 %scan.1 = bf16[32,8,640]{2,1,0:T(8,128)(2,1)} custom-call(s32[1]{0:T(128)} %bitcast.2.me, bf16[32,8,768]{2,1,0:T(8,128)(2,1)S(1)} %all-to-all-done.in_ref, bf16[128,640]{1,0:T(8,128)(2,1)S(1)} %copy-done), custom_call_target="tpu_custom_call" | custom-call | tf_op jit(solution)/shard_map/scan/pallas_call | solution.py:238
  53.6 5.2 %all-to-all-start.1 = ((bf16[32,8,640]{2,1,0:T(8,128)(2,1)}), bf16[32,8,640]{2,1,0:T(8,128)(2,1)S(1)}, u32[]{:S(2)}, u32[]{:S(2)}) async-start(bf16[32,8,640]{2,1,0:T(8,128)(2,1)} %scan.1), calls=%async_computation.1 | async-start | bytes 655360 | tf_op jit(solution)/shard_map/all_to_all | solution.py:564
  58.8 9.9 %chunk_chain.1 = (f32[2048,128]{1,0:T(8,128)}, f32[2048,128]{1,0:T(8,128)}, bf16[16,128,640]{2,1,0:T(8,128)(2,1)}) custom-call(bf16[2048,640]{1,0:T(8,128)(2,1)} %x_hbm.5, bf16[2048,640]{1,0:T(8,128)(2,1)} %g_hbm.5, bf16[2048,256]{1,0:T(8,128)(2,1)} %get-tuple-element.43.bc_hbm, bf16[2048,128]{1,0:T(8,128)(2,1)} %get-tuple-element.49.sc_hbm, ...), custom_call_target="tpu_custom_call" | custom-call | flops 4000000000 | bytes 16000000 | tf_op jit(solution)/shard_map/chunk_chain/pallas_call | solution.py:373
  68.6 2.5 %all-to-all-done.1 = bf16[32,8,640]{2,1,0:T(8,128)(2,1)S(1)} async-done(((bf16[32,8,640]{2,1,0:T(8,128)(2,1)}), bf16[32,8,640]{2,1,0:T(8,128)(2,1)S(1)}, u32[]{:S(2)}, u32[]{:S(2)}) %all-to-all-start.1) | async-done | bytes 327712 | tf_op jit(solution)/shard_map/all_to_all | solution.py:564
  71.1 4.4 %carry.1 = (f32[4,256,256]{2,1,0:T(8,128)S(1)}, bf16[4,256,256]{2,1,0:T(8,128)(2,1)S(1)}) custom-call(s32[2]{0:T(128)S(1)} %pad_add_fusion.place, bf16[2048,640]{1,0:T(8,128)(2,1)} %get-tuple-element.39.xt_hbm, bf16[2048,640]{1,0:T(8,128)(2,1)} %get-tuple-element.40.ge_hbm, f32[2048,128]{1,0:T(8,128)} %get-tuple-element.53.gb_hbm, ...), custom_call_target="tpu_custom_call" | custom-call | flops 700000000 | bytes 9000000 | tf_op jit(solution)/shard_map/carry/pallas_call | solution.py:426
  75.5 2.4 %collective-permute-start.7 = (bf16[4,256,256]{2,1,0:T(8,128)(2,1)S(1)}, bf16[4,256,256]{2,1,0:T(8,128)(2,1)S(1)}, u32[]{:S(2)}, u32[]{:S(2)}) collective-permute-start(bf16[4,256,256]{2,1,0:T(8,128)(2,1)S(1)} %get-tuple-element.56), channel_id=1, source_target_pairs={{0,1},{1,0},{2,3},{3,2},{4,5},{5,4},{6,7},{7,6},{8,9},{9,8},{10,11... | collective-permute-start | bytes 1572872 | tf_op jit(solution)/shard_map/ppermute | solution.py:567
  77.9 1.5 %collective-permute-done.7.got_ref = bf16[4,256,256]{2,1,0:T(8,128)(2,1)S(1)} collective-permute-done((bf16[4,256,256]{2,1,0:T(8,128)(2,1)S(1)}, bf16[4,256,256]{2,1,0:T(8,128)(2,1)S(1)}, u32[]{:S(2)}, u32[]{:S(2)}) %collective-permute-start.7) | collective-permute-done | bytes 524320 | tf_op jit(solution)/shard_map/ppermute | solution.py:567
  79.4 0.6 pair_sums.1
  80.1 1.7 %collective-permute-start.8 = (bf16[256,256]{1,0:T(8,128)(2,1)S(1)}, bf16[256,256]{1,0:T(8,128)(2,1)S(1)}, u32[]{:S(2)}, u32[]{:S(2)}) collective-permute-start(bf16[256,256]{1,0:T(8,128)(2,1)S(1)} %get-tuple-element.58), channel_id=1, source_target_pairs={{0,2},{1,3},{2,4},{3,5},{4,6},{5,7},{6,0},{7,1},{8,10},{9,11},{10,... | collective-permute-start | bytes 393224 | tf_op jit(solution)/shard_map/ppermute | solution.py:568
  81.8 1.6 %collective-permute-start.9 = (bf16[256,256]{1,0:T(8,128)(2,1)S(1)}, bf16[256,256]{1,0:T(8,128)(2,1)S(1)}, u32[]{:S(2)}, u32[]{:S(2)}) collective-permute-start(bf16[256,256]{1,0:T(8,128)(2,1)S(1)} %get-tuple-element.59), channel_id=1, source_target_pairs={{0,4},{1,5},{2,6},{3,7},{4,0},{5,1},{6,2},{7,3},{8,12},{9,13},{10,... | collective-permute-start | bytes 393224 | tf_op jit(solution)/shard_map/ppermute | solution.py:568
  83.3 0.9 %collective-permute-start.10 = (bf16[256,256]{1,0:T(8,128)(2,1)S(1)}, bf16[256,256]{1,0:T(8,128)(2,1)S(1)}, u32[]{:S(2)}, u32[]{:S(2)}) collective-permute-start(bf16[256,256]{1,0:T(8,128)(2,1)S(1)} %get-tuple-element.60), channel_id=1, source_target_pairs={{0,6},{1,7},{2,0},{3,1},{4,2},{5,3},{6,4},{7,5},{8,14},{9,15},{10,... | collective-permute-start | bytes 393224 | tf_op jit(solution)/shard_map/ppermute | solution.py:568
  84.3 4.9 %input_gradient.1 = bf16[2048,640]{1,0:T(8,128)(2,1)} custom-call(bf16[2048,640]{1,0:T(8,128)(2,1)} %get-tuple-element.48.gx_hbm, bf16[16,128,640]{2,1,0:T(8,128)(2,1)} %get-tuple-element.51.tst_hbm, bf16[2048,256]{1,0:T(8,128)(2,1)} %get-tuple-element.43.bc_hbm, bf16[2048,128]{1,0:T(8,128)(2,1)} %get-tuple-element.49.sc_hbm, bf16[256,640]{1,0:T(8,128)(2,1)S(1)} %bitcast.5, ...), custom_call_target="tpu_custom_call" | custom-call | flops 2000000000 | bytes 12000000 | tf_op jit(solution)/shard_map/input_gradient/pallas_call | solution.py:475
  89.2 0.2 collective-permute-done.9.c_ref
  89.4 0.7 totals.1
  (24 shorter events, 0.7 us)
Async XLA Ops:
  0.6 0.8 copy-start.2
  1.5 0.8 copy-start.3
  2.3 15.9 %collective-permute-start.2 = (bf16[256,256]{1,0:T(8,128)(2,1)S(1)}, bf16[256,256]{1,0:T(8,128)(2,1)S(1)}, u32[]{:S(2)}, u32[]{:S(2)}) collective-permute-start(bf16[256,256]{1,0:T(8,128)(2,1)S(1)} %join.1.m0), channel_id=1, source_target_pairs={{0,6},{1,7},{2,0},{3,1},{4,2},{5,3},{6,4},{7,5},{8,14},{9,15},{10,... | collective-permute-start | bytes 393224 | tf_op jit(solution)/shard_map/ppermute | solution.py:554
  6.0 12.3 %collective-permute-start.1 = (bf16[256,256]{1,0:T(8,128)(2,1)S(1)}, bf16[256,256]{1,0:T(8,128)(2,1)S(1)}, u32[]{:S(2)}, u32[]{:S(2)}) collective-permute-start(bf16[256,256]{1,0:T(8,128)(2,1)S(1)} %join.1.m0), channel_id=1, source_target_pairs={{0,4},{1,5},{2,6},{3,7},{4,0},{5,1},{6,2},{7,3},{8,12},{9,13},{10,... | collective-permute-start | bytes 393224 | tf_op jit(solution)/shard_map/ppermute | solution.py:554
  6.3 12.0 %collective-permute-start = (bf16[256,256]{1,0:T(8,128)(2,1)S(1)}, bf16[256,256]{1,0:T(8,128)(2,1)S(1)}, u32[]{:S(2)}, u32[]{:S(2)}) collective-permute-start(bf16[256,256]{1,0:T(8,128)(2,1)S(1)} %join.1.m0), channel_id=1, source_target_pairs={{0,2},{1,3},{2,4},{3,5},{4,6},{5,7},{6,0},{7,1},{8,10},{9,11},{10,... | collective-permute-start | bytes 393224 | tf_op jit(solution)/shard_map/ppermute | solution.py:554
  8.0 0.7 copy-start.4
  8.7 1.0 %copy-start.6 = (bf16[128,1280]{1,0:T(8,128)(2,1)S(1)}, bf16[128,1280]{1,0:T(8,128)(2,1)}, u32[]{:S(2)}) copy-start(bf16[128,1280]{1,0:T(8,128)(2,1)} %constant.26.clone.sp_ref) | copy-start | bytes 983044
  18.3 2.6 %collective-permute-start.3 = (bf16[256,256]{1,0:T(8,128)(2,1)S(1)}, bf16[256,256]{1,0:T(8,128)(2,1)S(1)}, u32[]{:S(2)}, u32[]{:S(2)}) collective-permute-start(bf16[256,256]{1,0:T(8,128)(2,1)S(1)} %join.1.m0), channel_id=1, source_target_pairs={{0,1},{1,0},{2,3},{3,2},{4,5},{5,4},{6,7},{7,6},{8,9},{9,8},{10,11... | collective-permute-start | bytes 393224 | tf_op jit(solution)/shard_map/ppermute | solution.py:557
  19.9 1.3 %collective-permute-start.4 = (bf16[256,256]{1,0:T(8,128)(2,1)S(1)}, bf16[256,256]{1,0:T(8,128)(2,1)S(1)}, u32[]{:S(2)}, u32[]{:S(2)}) collective-permute-start(bf16[256,256]{1,0:T(8,128)(2,1)S(1)} %collective-permute-done.m1), channel_id=1, source_target_pairs={{0,1},{1,0},{2,3},{3,2},{4,5},{5,4},{6,7},{7,6},{8,9},{9,8},{10,11... | collective-permute-start | bytes 393224 | tf_op jit(solution)/shard_map/ppermute | solution.py:557
  20.0 1.4 %collective-permute-start.5 = (bf16[256,256]{1,0:T(8,128)(2,1)S(1)}, bf16[256,256]{1,0:T(8,128)(2,1)S(1)}, u32[]{:S(2)}, u32[]{:S(2)}) collective-permute-start(bf16[256,256]{1,0:T(8,128)(2,1)S(1)} %collective-permute-done.1.m2), channel_id=1, source_target_pairs={{0,1},{1,0},{2,3},{3,2},{4,5},{5,4},{6,7},{7,6},{8,9},{9,8},{10,11... | collective-permute-start | bytes 393224 | tf_op jit(solution)/shard_map/ppermute | solution.py:557
  20.4 1.3 %collective-permute-start.6 = (bf16[256,256]{1,0:T(8,128)(2,1)S(1)}, bf16[256,256]{1,0:T(8,128)(2,1)S(1)}, u32[]{:S(2)}, u32[]{:S(2)}) collective-permute-start(bf16[256,256]{1,0:T(8,128)(2,1)S(1)} %collective-permute-done.2.m3), channel_id=1, source_target_pairs={{0,1},{1,0},{2,3},{3,2},{4,5},{5,4},{6,7},{7,6},{8,9},{9,8},{10,11... | collective-permute-start | bytes 393224 | tf_op jit(solution)/shard_map/ppermute | solution.py:557
  21.8 16.3 %copy-start.7 = (f32[10]{0:T(128)S(1)}, f32[10]{0:T(128)}, u32[]{:S(2)}) copy-start(f32[10]{0:T(128)} %param.14) | copy-start | bytes 124
  21.8 16.5 %copy-start.5 = (s32[1,4]{1,0:T(1,128)S(1)}, s32[1,4]{1,0:T(1,128)}, u32[]{:S(2)}) copy-start(s32[1,4]{1,0:T(1,128)} %off.3) | copy-start | bytes 52
  27.0 25.5 %all-to-all-start = ((bf16[32,8,768]{2,1,0:T(8,128)(2,1)}), bf16[32,8,768]{2,1,0:T(8,128)(2,1)S(1)}, u32[]{:S(2)}, u32[]{:S(2)}) async-start(bf16[32,8,768]{2,1,0:T(8,128)(2,1)} %get-tuple-element.42), calls=%async_computation | async-start | bytes 786432 | tf_op jit(solution)/shard_map/all_to_all | solution.py:559
  38.2 14.2 %copy-start = (bf16[128,640]{1,0:T(8,128)(2,1)S(1)}, bf16[128,640]{1,0:T(8,128)(2,1)}, u32[]{:S(2)}) copy-start(bf16[128,640]{1,0:T(8,128)(2,1)} %constant.28.clone.spf_ref.sp_ref) | copy-start | bytes 491524
  38.2 20.5 %copy-start.1 = (bf16[128,1280]{1,0:T(8,128)(2,1)S(1)}, bf16[128,1280]{1,0:T(8,128)(2,1)}, u32[]{:S(2)}) copy-start(bf16[128,1280]{1,0:T(8,128)(2,1)} %constant.27.clone.sp_ref) | copy-start | bytes 983044
  53.6 17.5 %all-to-all-start.1 = ((bf16[32,8,640]{2,1,0:T(8,128)(2,1)}), bf16[32,8,640]{2,1,0:T(8,128)(2,1)S(1)}, u32[]{:S(2)}, u32[]{:S(2)}) async-start(bf16[32,8,640]{2,1,0:T(8,128)(2,1)} %scan.1), calls=%async_computation.1 | async-start | bytes 655360 | tf_op jit(solution)/shard_map/all_to_all | solution.py:564
  75.5 3.9 %collective-permute-start.7 = (bf16[4,256,256]{2,1,0:T(8,128)(2,1)S(1)}, bf16[4,256,256]{2,1,0:T(8,128)(2,1)S(1)}, u32[]{:S(2)}, u32[]{:S(2)}) collective-permute-start(bf16[4,256,256]{2,1,0:T(8,128)(2,1)S(1)} %get-tuple-element.56), channel_id=1, source_target_pairs={{0,1},{1,0},{2,3},{3,2},{4,5},{5,4},{6,7},{7,6},{8,9},{9,8},{10,11... | collective-permute-start | bytes 1572872 | tf_op jit(solution)/shard_map/ppermute | solution.py:567
  80.1 9.1 %collective-permute-start.8 = (bf16[256,256]{1,0:T(8,128)(2,1)S(1)}, bf16[256,256]{1,0:T(8,128)(2,1)S(1)}, u32[]{:S(2)}, u32[]{:S(2)}) collective-permute-start(bf16[256,256]{1,0:T(8,128)(2,1)S(1)} %get-tuple-element.58), channel_id=1, source_target_pairs={{0,2},{1,3},{2,4},{3,5},{4,6},{5,7},{6,0},{7,1},{8,10},{9,11},{10,... | collective-permute-start | bytes 393224 | tf_op jit(solution)/shard_map/ppermute | solution.py:568
  81.8 7.6 %collective-permute-start.9 = (bf16[256,256]{1,0:T(8,128)(2,1)S(1)}, bf16[256,256]{1,0:T(8,128)(2,1)S(1)}, u32[]{:S(2)}, u32[]{:S(2)}) collective-permute-start(bf16[256,256]{1,0:T(8,128)(2,1)S(1)} %get-tuple-element.59), channel_id=1, source_target_pairs={{0,4},{1,5},{2,6},{3,7},{4,0},{5,1},{6,2},{7,3},{8,12},{9,13},{10,... | collective-permute-start | bytes 393224 | tf_op jit(solution)/shard_map/ppermute | solution.py:568
  83.3 6.1 %collective-permute-start.10 = (bf16[256,256]{1,0:T(8,128)(2,1)S(1)}, bf16[256,256]{1,0:T(8,128)(2,1)S(1)}, u32[]{:S(2)}, u32[]{:S(2)}) collective-permute-start(bf16[256,256]{1,0:T(8,128)(2,1)S(1)} %get-tuple-element.60), channel_id=1, source_target_pairs={{0,6},{1,7},{2,0},{3,1},{4,2},{5,3},{6,4},{7,5},{8,14},{9,15},{10,... | collective-permute-start | bytes 393224 | tf_op jit(solution)/shard_map/ppermute | solution.py:568

commit v2 on v1

--- a/solution.py
+++ b/solution.py
@@ -20,8 +20,8 @@
 BLOCK = 256
 BLOCKS = TOK // BLOCK
 VMEM = 28 * 1024 * 1024
-LOG2E = 1.4426950408889634
 NEG = -1e30
+AHEAD = 2
 
 
 def spread(first):
@@ -35,6 +35,7 @@
 SPREAD_D = np.concatenate([spread(0), spread(32)], axis=1)
 SPREAD_C = np.concatenate([spread(64), spread(96)], axis=1)
 SPREAD_F = spread(0)
+SUMS = np.concatenate([np.triu(np.ones((Q, Q))), np.tril(np.ones((Q, Q)), -1)], axis=1).astype(np.float32)
 
 
 def nt(a, b):
@@ -56,6 +57,14 @@
 
 def far(*arrays):
     return [pltpu.with_memory_space_constraint(a, pltpu.HBM) for a in arrays]
+
+
+def kept(shape, dtype):
+    return pltpu.VMEM(shape, dtype)
+
+
+def held(*arrays):
+    return [pltpu.with_memory_space_constraint(a, pltpu.VMEM) for a in arrays]
 
 
 def far_out(shape, dtype):
@@ -82,19 +91,30 @@
     return count
 
 
-def decay_part(off, l_ref, gain_ref, lg_ref, lrow_ref, lshift_ref, sc_ref, dec_ref):
-    lane = lax.broadcasted_iota(jnp.int32, (PAD, Q), 1)
-    rev = [None] * CHUNKS
-    fwd = [None] * CHUNKS
+def minus_expm1(y):
+    series = 1.0 + y * (1.0 / 10)
+    for n in range(9, 1, -1):
+        series = 1.0 + y * (1.0 / n) * series
+    return jnp.where(y > -0.5, -y * series, 1.0 - jnp.exp(y))
+
+
+def decay_part(off, l_ref, sums_ref, cum_ref, sc_ref, dec_ref):
+    extra = jnp.full((PAD - HEADS, Q), -1.0, F32)
+    pieces = []
     for c in range(CHUNKS):
-        x = l_ref[:, c * Q : (c + 1) * Q]
-        y, z = x, x
-        for k in (1, 2, 4, 8, 16, 32, 64):
-            y = y + jnp.where(lane >= k, pltpu.roll(y, k, 1), 0.0)
-            z = z + jnp.where(lane < Q - k, pltpu.roll(z, Q - k, 1), 0.0)
-        fwd[c] = y
-        rev[c] = jnp.where(lane < Q - 1, pltpu.roll(z, Q - 1, 1), 0.0)
-    ends = [fwd[c][:, Q - 1 : Q] for c in range(CHUNKS)]
+        pieces += [l_ref[:, c * Q : (c + 1) * Q], extra]
+    l = jnp.concatenate(pieces, axis=0)
+    square = jnp.maximum(minus_expm1(2.0 * l), 1.2e-38)
+    gain = jnp.sqrt(square)
+    lg = jnp.log(square) * 0.5
+    high = l.astype(BF16)
+    rest = l - high.astype(F32)
+    mid = rest.astype(BF16)
+    low = (rest - mid.astype(F32)).astype(BF16)
+    both = nn(high, sums_ref[...]) + nn(mid, sums_ref[...]) + nn(low, sums_ref[...])
+    fwd, rev = both[:, :Q], both[:, Q:]
+    cut = lambda a, c: a[c * PAD : (c + 1) * PAD]
+    ends = [cut(fwd, c)[:, Q - 1 : Q] for c in range(CHUNKS)]
     before = [jnp.zeros((PAD, 1), F32)]
     for c in range(CHUNKS):
         before.append(before[-1] + ends[c])
@@ -103,121 +123,169 @@
         after.append(after[-1] + ends[c])
     after = after[::-1]
     last_count = starts_until(off, jnp.int32(TOK - 1))
+    lane = lax.broadcasted_iota(jnp.int32, (PAD, Q), 1)
     decs = jnp.zeros((PAD, Q), F32)
+    tail = jnp.exp(rev) * gain
+    entry = jnp.exp(fwd)
+    shift = fwd - lg
     for c in range(CHUNKS):
-        t = lane + c * Q
-        seg = starts_until(off, t)
+        seg = starts_until(off, lane + c * Q)
         seg_b = starts_until(off, jnp.int32(c * Q - 1))
         seg_e = starts_until(off, jnp.int32(c * Q + Q - 1))
-        gain = gain_ref[:, c * Q : (c + 1) * Q]
-        tail_d = jnp.where(seg == last_count, jnp.exp2(rev[c] + after[c]) * gain, 0.0)
-        entry_d = jnp.where(seg == 0, jnp.exp2(fwd[c] + before[c]), 0.0)
-        tail_c = jnp.where(seg == seg_e, jnp.exp2(rev[c]) * gain, 0.0)
-        entry_c = jnp.where(seg == seg_b, jnp.exp2(fwd[c]), 0.0)
+        tail_c = jnp.where(seg == seg_e, cut(tail, c), 0.0)
+        entry_c = jnp.where(seg == seg_b, cut(entry, c), 0.0)
+        tail_d = jnp.where(seg == last_count, jnp.exp(cut(rev, c) + after[c]) * cut(gain, c), 0.0)
+        entry_d = jnp.where(seg == 0, jnp.exp(cut(fwd, c) + before[c]), 0.0)
         rows = []
-        for v in (tail_d, entry_d, tail_c, entry_c):
-            hi = v.astype(BF16).astype(F32)
-            rows += [hi, v - hi]
-        sc_ref[c * Q : (c + 1) * Q, :] = jnp.concatenate(rows, axis=0).T.astype(BF16)
-        lrow_ref[:, c * Q : (c + 1) * Q] = fwd[c]
-        lshift_ref[:, c * Q : (c + 1) * Q] = fwd[c] - lg_ref[:, c * Q : (c + 1) * Q]
+        for a in (tail_d, entry_d, tail_c, entry_c):
+            hi = a.astype(BF16)
+            rows += [hi, (a - hi.astype(F32)).astype(BF16)]
+        sc_ref[c * Q : (c + 1) * Q, :] = jnp.concatenate(rows, axis=0).T
+        cum_ref[:PAD, c * Q : (c + 1) * Q] = cut(fwd, c)
+        cum_ref[PAD:, c * Q : (c + 1) * Q] = cut(shift, c)
         keep_c = jnp.where(seg_b == seg_e, 1.0, 0.0)
-        decs = jnp.where(lane == c, jnp.exp2(ends[c]) * keep_c, decs)
+        decs = jnp.where(lane == c, jnp.exp(ends[c]) * keep_c, decs)
         keep_after = jnp.where(seg_e == last_count, 1.0, 0.0)
-        decs = jnp.where(lane == 32 + c, jnp.exp2(after[c]) * keep_after, decs)
+        decs = jnp.where(lane == 32 + c, jnp.exp(after[c]) * keep_after, decs)
     keep = jnp.where(last_count == 0, 1.0, 0.0)
-    decs = jnp.where(lane == CHUNKS, jnp.exp2(before[CHUNKS]) * keep, decs)
+    decs = jnp.where(lane == CHUNKS, jnp.exp(before[CHUNKS]) * keep, decs)
     hi = decs.astype(BF16).astype(F32)
     full = jnp.concatenate([hi, decs - hi, jnp.zeros((Q - 2 * PAD, Q), F32)], axis=0)
     dec_ref[...] = full.T.astype(BF16)
 
 
 def prepare_kernel(
-    off, l_ref, gain_ref, lg_ref, x_hbm, g_hbm, sp_ref,
-    lrow_ref, lshift_ref, sc_ref, dec_ref, xt_hbm, ge_hbm, x_ref, g_ref, in_sem, out_sem,
+    off_hbm, l_hbm, sums_hbm, sp_hbm, x_hbm, g_hbm, cum_hbm, sc_hbm, dec_hbm, xt_ref, xt_hbm, ge_hbm,
+    off, l_ref, sums_ref, sp_ref, ge_ref, cum_ref, sc_ref, dec_ref, in_sem, first_sem, out_sem, ge_sem,
 ):
+    first = [
+        pltpu.make_async_copy(src, dst, first_sem.at[n])
+        for n, (src, dst) in enumerate(((l_hbm, l_ref), (off_hbm, off), (sums_hbm, sums_ref), (sp_hbm, sp_ref)))
+    ]
+    for copy in first:
+        copy.start()
     for i in range(BLOCKS):
-        block_copy(x_hbm, x_ref, in_sem, 0, i).start()
-        block_copy(g_hbm, g_ref, in_sem, 1, i).start()
-    decay_part(off, l_ref, gain_ref, lg_ref, lrow_ref, lshift_ref, sc_ref, dec_ref)
+        block_copy(x_hbm, xt_ref, in_sem, 0, i).start()
+        block_copy(g_hbm, ge_ref, in_sem, 1, i).start()
+    for copy in first:
+        copy.wait()
+    decay_part(off, l_ref, sums_ref, cum_ref, sc_ref, dec_ref)
+    saves = [
+        pltpu.make_async_copy(src, dst, out_sem.at[n])
+        for n, (src, dst) in enumerate(((cum_ref, cum_hbm), (sc_ref, sc_hbm), (dec_ref, dec_hbm)))
+    ]
+    for save in saves:
+        save.start()
 
     @pl.loop(0, BLOCKS)
     def _(i):
-        block_copy(x_hbm, x_ref, in_sem, 0, i).wait()
-        block_copy(g_hbm, g_ref, in_sem, 1, i).wait()
+        block_copy(x_hbm, xt_ref, in_sem, 0, i).wait()
+        block_copy(g_hbm, ge_ref, in_sem, 1, i).wait()
         r = pl.ds(pl.multiple_of(i * BLOCK, BLOCK), BLOCK)
         s = nn(sc_ref[r, :], sp_ref[...])
-        x_ref[r, :] = (x_ref[r, :].astype(F32) * s[:, :WIDTH]).astype(BF16)
-        g_ref[r, :] = (g_ref[r, :].astype(F32) * s[:, WIDTH:]).astype(BF16)
-        block_copy(x_ref, xt_hbm, out_sem, 0, i).start()
-        block_copy(g_ref, ge_hbm, out_sem, 1, i).start()
-
+        ge_ref[r, :] = (ge_ref[r, :].astype(F32) * s[:, WIDTH:]).astype(BF16)
+        block_copy(ge_ref, ge_hbm, ge_sem, 0, i).start()
+        xt_ref[r, :] = (xt_ref[r, :].astype(F32) * s[:, :WIDTH]).astype(BF16)
+        block_copy(xt_ref, xt_hbm, ge_sem, 1, i).start()
+
+    for save in saves:
+        save.wait()
     for i in range(BLOCKS):
-        block_copy(x_ref, xt_hbm, out_sem, 0, i).wait()
-        block_copy(g_ref, ge_hbm, out_sem, 1, i).wait()
-
-
-def prepare_call(off, log_decay, x, g, sp):
-    l = jnp.pad(log_decay, ((0, PAD - HEADS), (0, 0)), constant_values=-1.0)
-    square = -jnp.expm1(2.0 * l)
+        block_copy(ge_ref, ge_hbm, ge_sem, 0, i).wait()
+        block_copy(xt_ref, xt_hbm, ge_sem, 1, i).wait()
+
+
+def prepare_call(off, log_decay, sums, sp, x, g):
     return pl.pallas_call(
         prepare_kernel,
         out_shape=(
-            jax.ShapeDtypeStruct((PAD, TOK), F32),
-            jax.ShapeDtypeStruct((PAD, TOK), F32),
+            far_out((2 * PAD, TOK), F32),
             far_out((TOK, STATE), BF16),
-            jax.ShapeDtypeStruct((STATE, STATE), BF16),
+            far_out((STATE, STATE), BF16),
+            kept((TOK, WIDTH), BF16),
             far_out((TOK, WIDTH), BF16),
             far_out((TOK, WIDTH), BF16),
         ),
-        in_specs=[SCALARS, WHOLE, WHOLE, WHOLE, FAR, FAR, WHOLE],
-        out_specs=(WHOLE,) * 4 + (FAR,) * 2,
-        scratch_shapes=[pltpu.VMEM((TOK, WIDTH), BF16)] * 2 + [pltpu.SemaphoreType.DMA((2, BLOCKS))] * 2,
+        in_specs=[FAR] * 6,
+        out_specs=(FAR, FAR, FAR, WHOLE, FAR, FAR),
+        scratch_shapes=[
+            pltpu.SMEM((1, 4), jnp.int32),
+            pltpu.VMEM((HEADS, TOK), F32),
+            pltpu.VMEM((Q, 2 * Q), BF16),
+            pltpu.VMEM((STATE, 2 * WIDTH), BF16),
+            pltpu.VMEM((TOK, WIDTH), BF16),
+            pltpu.VMEM((2 * PAD, TOK), F32),
+            pltpu.VMEM((TOK, STATE), BF16),
+            pltpu.VMEM((STATE, STATE), BF16),
+            pltpu.SemaphoreType.DMA((2, BLOCKS)),
+            pltpu.SemaphoreType.DMA((4,)),
+            pltpu.SemaphoreType.DMA((3,)),
+            pltpu.SemaphoreType.DMA((2, BLOCKS)),
+        ],
         compiler_params=options(),
         cost_estimate=cost(4e9, 16e6),
         name="prepare",
-    )(off, l * LOG2E, jnp.sqrt(square), 0.5 * jnp.log2(square), *far(x, g), sp)
+    )(*far(off, log_decay, sums, sp, x, g))
 
 
 def state_kernel(
-    place, m0, m1, m2, m3, o0, o1, o2, o3, xt_hbm, ge_hbm, dec_ref, out_ref, bc_hbm,
-    xt_ref, ge_ref, bc_ref, in_sem, out_sem,
+    place, m0, m1, m2, m3, o0, o1, o2, o3, xt_ref, ge_hbm, dec_hbm, out_ref, bc_hbm,
+    ge_ref, bc_ref, dec_ref, s_ref, in_sem, out_sem,
 ):
-    rows = TOK // 4
-    for i in range(4):
-        block_copy(xt_hbm, xt_ref, in_sem, 0, i, rows).start()
-        block_copy(ge_hbm, ge_ref, in_sem, 1, i, rows).start()
+    load = pltpu.make_async_copy(ge_hbm, ge_ref, in_sem.at[0])
+    load.start()
+    dec_load = pltpu.make_async_copy(dec_hbm, dec_ref, in_sem.at[1])
+    dec_load.start()
     core, y = place[0], place[1]
     for k, (m, o) in enumerate(((m0, o0), (m1, o1), (m2, o2), (m3, o3))):
         pair = lax.rem(y + 4 - k, 4) * 2
         bc_ref[pl.ds(pl.multiple_of((pair + core) * BLOCK, BLOCK), BLOCK), :] = m[...]
         bc_ref[pl.ds(pl.multiple_of((pair + 1 - core) * BLOCK, BLOCK), BLOCK), :] = o[...]
-    save = pltpu.make_async_copy(bc_ref, bc_hbm, out_sem)
-    save.start()
-    for i in range(4):
-        block_copy(xt_hbm, xt_ref, in_sem, 0, i, rows).wait()
-        block_copy(ge_hbm, ge_ref, in_sem, 1, i, rows).wait()
-    s = nn(bc_ref[:, :STATE].T, xt_ref[...])
-    out_ref[:16, :, :WIDTH] = s.reshape(16, 8, WIDTH).astype(BF16)
-    t = nn(bc_ref[:, STATE:].T, ge_ref[...])
-    out_ref[16:, :, :WIDTH] = t.reshape(16, 8, WIDTH).astype(BF16)
+    saves = [
+        pltpu.make_async_copy(src, dst, out_sem.at[n])
+        for n, (src, dst) in enumerate(((bc_ref, bc_hbm),))
+    ]
+    for save in saves:
+        save.start()
+    rows = TOK // 4
+    for first, src, half in ((0, xt_ref, slice(0, STATE)), (16, ge_ref, slice(STATE, 2 * STATE))):
+        if first:
+            load.wait()
+            dec_load.wait()
+        for i in range(4):
+            part = tn(bc_ref[i * rows : (i + 1) * rows, half], src[i * rows : (i + 1) * rows, :])
+            if i == 0:
+                s_ref[...] = part
+            else:
+                s_ref[...] += part
+        out_ref[first : first + 16, :, :WIDTH] = s_ref[...].reshape(16, 8, WIDTH).astype(BF16)
     row = dec_ref[CHUNKS : CHUNKS + 1, :].astype(F32)
     out_ref[:, :, WIDTH:] = jnp.broadcast_to(row[None], (32, 8, STATE)).astype(BF16)
-    save.wait()
+    for save in saves:
+        save.wait()
 
 
 def state_call(place, pieces, xt, ge, dec):
     return pl.pallas_call(
         state_kernel,
-        out_shape=(jax.ShapeDtypeStruct((32, 8, WIDTH + STATE), BF16), far_out((TOK, 2 * STATE), BF16)),
-        in_specs=[SCALARS] + [WHOLE] * 8 + [FAR, FAR, WHOLE],
+        out_shape=(
+            jax.ShapeDtypeStruct((32, 8, WIDTH + STATE), BF16),
+            far_out((TOK, 2 * STATE), BF16),
+        ),
+        in_specs=[SCALARS] + [WHOLE] * 9 + [FAR, FAR],
         out_specs=(WHOLE, FAR),
-        scratch_shapes=[pltpu.VMEM((TOK, WIDTH), BF16)] * 2
-        + [pltpu.VMEM((TOK, 2 * STATE), BF16), pltpu.SemaphoreType.DMA((2, 4)), pltpu.SemaphoreType.DMA],
+        scratch_shapes=[
+            pltpu.VMEM((TOK, WIDTH), BF16),
+            pltpu.VMEM((TOK, 2 * STATE), BF16),
+            pltpu.VMEM((STATE, STATE), BF16),
+            pltpu.VMEM((STATE, WIDTH), F32),
+            pltpu.SemaphoreType.DMA((2,)),
+            pltpu.SemaphoreType.DMA((2,)),
+        ],
         compiler_params=options(),
         cost_estimate=cost(7e8, 6.5e6),
         name="states",
-    )(place, *pieces, *far(xt, ge), dec)
+    )(place, *pieces, *held(xt), *far(ge, dec))
 
 
 def scan_kernel(me, in_ref, sp_ref, out_ref, d_ref):
@@ -247,46 +315,61 @@
 
 
 def within_kernel(
-    off, x_hbm, g_hbm, bc_hbm, lrow_ref, lshift_ref, skip_ref, gx_hbm, z_hbm,
-    x_ref, g_ref, bc_ref, gx_ref, z_ref, in_sem, out_sem,
+    off_hbm, x_hbm, g_hbm, bc_hbm, cum_hbm, skip_ref, gx_hbm, z_hbm,
+    off, cum_ref, x_ref, g_ref, bc_ref, gx_ref, z_ref, first_sem, in_sem, out_sem,
 ):
-    for i in range(BLOCKS):
+    first = [
+        pltpu.make_async_copy(off_hbm, off, first_sem.at[0]),
+        pltpu.make_async_copy(cum_hbm, cum_ref, first_sem.at[1]),
+    ]
+    for copy in first:
+        copy.start()
+    def fetch(i):
         block_copy(bc_hbm, bc_ref, in_sem, 2, i).start()
         block_copy(x_hbm, x_ref, in_sem, 0, i).start()
         block_copy(g_hbm, g_ref, in_sem, 1, i).start()
+
+    for i in range(AHEAD):
+        fetch(i)
     si = lax.broadcasted_iota(jnp.int32, (Q, Q), 0)
     ti = lax.broadcasted_iota(jnp.int32, (Q, Q), 1)
     even = lax.broadcasted_iota(jnp.int32, (Q, Q), 1) < 64
     odd = jnp.logical_not(even)
     zero = jnp.zeros((Q, Q), BF16)
+    for copy in first:
+        copy.wait()
 
     @pl.loop(0, BLOCKS)
     def _(step):
+        @pl.when(step + AHEAD < BLOCKS)
+        def _():
+            fetch(step + AHEAD)
+
         block_copy(bc_hbm, bc_ref, in_sem, 2, step).wait()
         block_copy(x_hbm, x_ref, in_sem, 0, step).wait()
         block_copy(g_hbm, g_ref, in_sem, 1, step).wait()
+        parts = []
         for sub in range(BLOCK // Q):
             base = pl.multiple_of(step * BLOCK + sub * Q, Q)
             r = pl.ds(base, Q)
             same = starts_until(off, si + base) == starts_until(off, ti + base)
             bias = jnp.where((ti >= si) & same, 0.0, NEG)
-            lt = lrow_ref[:, r]
-            ls = lshift_ref[:, r].T
-            scores = nt(bc_ref[r, :STATE], bc_ref[r, STATE:])
-            z = jnp.zeros((Q, Q), F32)
-            for p in range(HEADS // 2):
-                w = slice(p * Q, (p + 1) * Q)
-                x = x_ref[r, w]
+            parts.append((r, cum_ref[:PAD, r], cum_ref[PAD:, r].T, nt(bc_ref[r, :STATE], bc_ref[r, STATE:]), bias))
+        zs = [jnp.zeros((Q, Q), F32)] * len(parts)
+        for p in range(HEADS // 2):
+            w = slice(p * Q, (p + 1) * Q)
+            h = 2 * p
+            for n, (r, lt, ls, scores, bias) in enumerate(parts):
                 g = g_ref[r, w]
-                e = nt(jnp.concatenate([jnp.where(even, x, zero), jnp.where(odd, x, zero)], axis=0), g)
-                h = 2 * p
-                ma = jnp.exp2(lt[h : h + 1, :] - ls[:, h : h + 1] + bias)
-                mb = jnp.exp2(lt[h + 1 : h + 2, :] - ls[:, h + 1 : h + 2] + bias)
-                z = z + (ma * e[:Q] + mb * e[Q:])
+                both = jnp.concatenate([jnp.where(even, g, zero), jnp.where(odd, g, zero)], axis=0)
+                e = nt(x_ref[r, w], both)
+                ma = jnp.exp(lt[h : h + 1, :] - ls[:, h : h + 1] + bias)
+                mb = jnp.exp(lt[h + 1 : h + 2, :] - ls[:, h + 1 : h + 2] + bias)
+                zs[n] = zs[n] + (ma * e[:, :Q] + mb * e[:, Q:])
                 weights = jnp.concatenate([(ma * scores).astype(BF16), (mb * scores).astype(BF16)], axis=1)
-                both = jnp.concatenate([jnp.where(even, g, zero), jnp.where(odd, g, zero)], axis=0)
                 gx_ref[r, w] = (nn(weights, both) + g.astype(F32) * skip_ref[:, w]).astype(BF16)
-            z_ref[r, :] = z.astype(BF16)
+        for n, part in enumerate(parts):
+            z_ref[part[0], :] = zs[n].astype(BF16)
         block_copy(gx_ref, gx_hbm, out_sem, 0, step).start()
         block_copy(z_ref, z_hbm, out_sem, 1, step).start()
 
@@ -295,45 +378,48 @@
         block_copy(z_ref, z_hbm, out_sem, 1, i).wait()
 
 
-def within_call(off, x, g, bc, lrow, lshift, skip):
+def within_call(off, x, g, bc, cum, skip):
     return pl.pallas_call(
         within_kernel,
         out_shape=(far_out((TOK, WIDTH), BF16), far_out((TOK, STATE), BF16)),
-        in_specs=[SCALARS, FAR, FAR, FAR, WHOLE, WHOLE, WHOLE],
+        in_specs=[FAR] * 5 + [WHOLE],
         out_specs=(FAR, FAR),
         scratch_shapes=[
+            pltpu.SMEM((1, 4), jnp.int32),
+            pltpu.VMEM((2 * PAD, TOK), F32),
             pltpu.VMEM((TOK, WIDTH), BF16),
             pltpu.VMEM((TOK, WIDTH), BF16),
             pltpu.VMEM((TOK, 2 * STATE), BF16),
             pltpu.VMEM((TOK, WIDTH), BF16),
             pltpu.VMEM((TOK, STATE), BF16),
+            pltpu.SemaphoreType.DMA((2,)),
             pltpu.SemaphoreType.DMA((3, BLOCKS)),
             pltpu.SemaphoreType.DMA((2, BLOCKS)),
         ],
         compiler_params=options(),
         cost_estimate=cost(4e9, 16e6),
         name="within_chunks",
-    )(off, *far(x, g, bc), lrow, lshift, skip)
+    )(*far(off, x, g, bc, cum), skip)
 
 
 def chain_kernel(
-    x_hbm, g_hbm, bc_hbm, sc_hbm, z_hbm, dec_ref, sp_ref, spf_ref, gc_hbm, gb_hbm, tst_hbm,
-    x_ref, g_ref, bc_ref, sc_ref, z_ref, gc_ref, gb_ref, tst_ref, s_ref, t_ref, d_ref, in_sem, out_sem,
+    x_hbm, g_hbm, bc_hbm, sc_hbm, z_hbm, xt_hbm, dec_ref, sp_ref, spf_ref, gc_hbm, gb_hbm, tst_hbm, xt_ref,
+    x_ref, g_ref, bc_ref, sc_ref, z_ref, gc_ref, gb_ref, tst_ref, s_ref, t_ref, d_ref, in_sem, out_sem, next_sem,
 ):
     loads = ((sc_hbm, sc_ref), (x_hbm, x_ref), (g_hbm, g_ref), (bc_hbm, bc_ref), (z_hbm, z_ref))
     for i in range(BLOCKS // 2):
         for j in (i, BLOCKS - 1 - i):
             for n, (src, dst) in enumerate(loads):
                 block_copy(src, dst, in_sem, n, j).start()
+    ahead = pltpu.make_async_copy(xt_hbm, xt_ref, next_sem)
+    ahead.start()
     s_ref[...] = jnp.zeros_like(s_ref)
     t_ref[...] = jnp.zeros_like(t_ref)
     d_ref[...] = nn(dec_ref[:CHUNKS, :], spf_ref[...])
     per = BLOCK // Q
 
-    @pl.loop(0, BLOCKS)
-    def _(step):
-        @pl.when(step < BLOCKS // 2)
-        def _():
+    def advance(step, fresh):
+        if fresh:
             for j in (step, BLOCKS - 1 - step):
                 for n, (src, dst) in enumerate(loads):
                     block_copy(src, dst, in_sem, n, j).wait()
@@ -363,22 +449,32 @@
         block_copy(gb_ref, gb_hbm, out_sem, 1, back).start()
         block_copy(tst_ref, tst_hbm, out_sem, 2, back, per).start()
 
+    @pl.loop(0, BLOCKS // 2)
+    def _(step):
+        advance(step, True)
+
+    @pl.loop(BLOCKS // 2, BLOCKS)
+    def _(step):
+        advance(step, False)
+
     for i in range(BLOCKS):
         block_copy(gc_ref, gc_hbm, out_sem, 0, i).wait()
         block_copy(gb_ref, gb_hbm, out_sem, 1, i).wait()
         block_copy(tst_ref, tst_hbm, out_sem, 2, i, per).wait()
-
-
-def chain_call(x, g, bc, sc, z, dec, sp, spf):
+    ahead.wait()
+
+
+def chain_call(x, g, bc, sc, z, xt, dec, sp, spf):
     return pl.pallas_call(
         chain_kernel,
         out_shape=(
             far_out((TOK, STATE), F32),
             far_out((TOK, STATE), F32),
             far_out((CHUNKS, STATE, WIDTH), BF16),
+            kept((TOK, WIDTH), BF16),
         ),
-        in_specs=[FAR] * 5 + [WHOLE] * 3,
-        out_specs=(FAR,) * 3,
+        in_specs=[FAR] * 6 + [WHOLE] * 3,
+        out_specs=(FAR, FAR, FAR, WHOLE),
         scratch_shapes=[
             pltpu.VMEM((TOK, WIDTH), BF16),
             pltpu.VMEM((TOK, WIDTH), BF16),
@@ -393,32 +489,34 @@
             pltpu.VMEM((CHUNKS, WIDTH), F32),
             pltpu.SemaphoreType.DMA((5, BLOCKS)),
             pltpu.SemaphoreType.DMA((3, BLOCKS)),
+            pltpu.SemaphoreType.DMA,
         ],
         compiler_params=options(),
         cost_estimate=cost(4e9, 16e6),
         name="chunk_chain",
-    )(*far(x, g, bc, sc, z), dec, sp, spf)
-
-
-def carry_kernel(
-    place, xt_hbm, ge_hbm, gb_hbm, gc_hbm, st_ref, keep_ref, send_ref, xt_ref, ge_ref, gb_ref, gc_ref, in_sem
-):
+    )(*far(x, g, bc, sc, z, xt), dec, sp, spf)
+
+
+def carry_kernel(place, xt_ref, ge_hbm, gb_hbm, gc_hbm, st_ref, keep_ref, send_ref, ge_ref, gb_ref, gc_ref, in_sem):
     core = place[0]
-    loads = ((xt_hbm, xt_ref), (ge_hbm, ge_ref), (gb_hbm, gb_ref), (gc_hbm, gc_ref))
-    for i in range(BLOCKS):
-        for n, (src, dst) in enumerate(loads):
-            block_copy(src, dst, in_sem, n, i).start()
+    loads = ((gb_hbm, gb_ref), (gc_hbm, gc_ref), (ge_hbm, ge_ref))
+    for n, (src, dst) in enumerate(loads):
+        for i in range(4):
+            block_copy(src, dst, in_sem, n, i, 2 * BLOCK).start()
     s = st_ref[:STATE, :]
     t = st_ref[STATE:, :]
     for i in range(4):
-        for n, (src, dst) in enumerate(loads):
-            block_copy(src, dst, in_sem, n, 2 * i).wait()
-            block_copy(src, dst, in_sem, n, 2 * i + 1).wait()
+        block_copy(gb_hbm, gb_ref, in_sem, 0, i, 2 * BLOCK).wait()
         r = pl.ds(pl.multiple_of((2 * i + core) * BLOCK, BLOCK), BLOCK)
         keep_ref[i, :, :STATE] = gb_ref[r, :] + nt(xt_ref[r, :], t)
+        r = pl.ds(pl.multiple_of((2 * i + 1 - core) * BLOCK, BLOCK), BLOCK)
+        send_ref[i, :, :STATE] = (gb_ref[r, :] + nt(xt_ref[r, :], t)).astype(BF16)
+    for i in range(4):
+        block_copy(gc_hbm, gc_ref, in_sem, 1, i, 2 * BLOCK).wait()
+        block_copy(ge_hbm, ge_ref, in_sem, 2, i, 2 * BLOCK).wait()
+        r = pl.ds(pl.multiple_of((2 * i + core) * BLOCK, BLOCK), BLOCK)
         keep_ref[i, :, STATE:] = gc_ref[r, :] + nt(ge_ref[r, :], s)
         r = pl.ds(pl.multiple_of((2 * i + 1 - core) * BLOCK, BLOCK), BLOCK)
-        send_ref[i, :, :STATE] = (gb_ref[r, :] + nt(xt_ref[r, :], t)).astype(BF16)
         send_ref[i, :, STATE:] = (gc_ref[r, :] + nt(ge_ref[r, :], s)).astype(BF16)
 
 
@@ -429,19 +527,18 @@
             jax.ShapeDtypeStruct((4, BLOCK, 2 * STATE), F32),
             jax.ShapeDtypeStruct((4, BLOCK, 2 * STATE), BF16),
         ),
-        in_specs=[SCALARS] + [FAR] * 4 + [WHOLE],
+        in_specs=[SCALARS, WHOLE, FAR, FAR, FAR, WHOLE],
         out_specs=(WHOLE, WHOLE),
         scratch_shapes=[
             pltpu.VMEM((TOK, WIDTH), BF16),
-            pltpu.VMEM((TOK, WIDTH), BF16),
             pltpu.VMEM((TOK, STATE), F32),
             pltpu.VMEM((TOK, STATE), F32),
-            pltpu.SemaphoreType.DMA((4, BLOCKS)),
+            pltpu.SemaphoreType.DMA((3, 4)),
         ],
         compiler_params=options(),
         cost_estimate=cost(7e8, 9e6),
         name="carry",
-    )(place, *far(xt, ge, gb, gc), st)
+    )(place, *held(xt), *far(ge, gb, gc), st)
 
 
 def input_kernel(
@@ -492,15 +589,27 @@
     )(*far(gx, tst, bc, sc), st, sp, dec, spf)
 
 
-def join_kernel(a_ref, b_ref, out_ref):
-    out_ref[:, :STATE] = a_ref[...]
-    out_ref[:, STATE:] = b_ref[...]
+def join_kernel(a_hbm, b_hbm, out_ref, sem):
+    loads = [
+        pltpu.make_async_copy(a_hbm, out_ref.at[:, :STATE], sem.at[0]),
+        pltpu.make_async_copy(b_hbm, out_ref.at[:, STATE:], sem.at[1]),
+    ]
+    for load in loads:
+        load.start()
+    for load in loads:
+        load.wait()
 
 
 def join_call(a, b):
     return pl.pallas_call(
-        join_kernel, out_shape=jax.ShapeDtypeStruct((BLOCK, 2 * STATE), BF16), compiler_params=options(), name="join"
-    )(a, b)
+        join_kernel,
+        out_shape=jax.ShapeDtypeStruct((BLOCK, 2 * STATE), BF16),
+        in_specs=[FAR, FAR],
+        out_specs=WHOLE,
+        scratch_shapes=[pltpu.SemaphoreType.DMA((2,))],
+        compiler_params=options(),
+        name="join",
+    )(*far(a, b))
 
 
 def pair_kernel(place, keep_ref, got_ref, o0, o1, o2, o3):
@@ -552,17 +661,21 @@
     spread_d, spread_c, spread_f = (jnp.asarray(a, BF16) for a in (SPREAD_D, SPREAD_C, SPREAD_F))
     own = join_call(write_rows, read_rows)
     mine = [own] + [lax.ppermute(own, "head", along_y(k)) for k in (1, 2, 3)]
-    lrow, lshift, sc, dec, xt, ge = prepare_call(reset_offsets, log_decay, mixer_input, grad_out, spread_d)
+    cum, sc, dec, xt, xt_far, ge = prepare_call(
+        reset_offsets, log_decay, jnp.asarray(SUMS, BF16), spread_d, mixer_input, grad_out
+    )
     *mine, xt, ge = lax.optimization_barrier((*mine, xt, ge))
     other = [lax.ppermute(a, "head", SWAP) for a in mine]
     payload, bc = state_call(place, mine + other, xt, ge, dec)
     parts = lax.all_to_all(payload, "seq", 0, 0, tiled=True)
     skip = jnp.repeat(skip_gain, 64)[None, :]
-    gx, z = within_call(reset_offsets, mixer_input, grad_out, bc, lrow, lshift, skip)
+    gx, z = within_call(reset_offsets, mixer_input, grad_out, bc, cum, skip)
     parts, gx, z = lax.optimization_barrier((parts, gx, z))
     entering = scan_call(me, parts, spread_f)
     st = lax.all_to_all(entering, "seq", 0, 0, tiled=True).reshape(2 * STATE, WIDTH)
-    gc, gb, tst = chain_call(mixer_input, grad_out, bc, sc, z, dec, spread_c, spread_f)
+    gc, gb, tst, xt = chain_call(
+        mixer_input, grad_out, bc, sc, z, xt_far, dec, spread_c, spread_f
+    )
     keep, send = carry_call(place, xt, ge, gb, gc, st)
     total, *leaving = pair_call(place, keep, lax.ppermute(send, "head", SWAP))
     arrived = [lax.ppermute(a, "head", along_y(k)) for k, a in zip((1, 2, 3), leaving)]

time: 90.6 us -> 84.8 us (0.936)
  local copies, waits for them, and re-layouts: 3.46 us -> 0.16 us
  Pallas kernels: 45.5 us -> 43 us
  waiting for transfers between devices: 9.65 us -> 11.4 us
  other arithmetic: 1.08 us -> 0.07 us
    unnamed x16 -> x8, local copies, waits for them, and re-layouts: 3.31 us -> 0.01 us
    pallas_call x1, Pallas kernels: 8.59 us -> 7.02 us  [prepare_call(): pl.pallas_call(prepare_kernel, out_shape=(far_out((2 * PAD, TOK), F32), f...]
    ppermute x1, starting transfers between devices: 2.39 us -> 3.92 us  [shards(): total, *leaving = pair_call(place, keep, lax.ppermute(send, 'head', SWAP))]
    ppermute x3, waiting for transfers between devices: 0.01 us -> 1.54 us  [shards(): mine = [own] + [lax.ppermute(own, 'head', along_y(k)) for k in (1, 2, 3)]]
    all_to_all x1, waiting for transfers between devices: 2.49 us -> 1.27 us  [shards(): lax.all_to_all(entering, 'seq', 0, 0, tiled=True).reshape(2 * STATE, WIDTH)]
    ppermute x4, starting transfers between devices: 2.21 us -> 1.12 us  [shards(): other = [lax.ppermute(a, 'head', SWAP) for a in mine]]
    mul x1 -> x0, other arithmetic: 1.01 us -> none  [prepare_call(): 0.5 * jnp.log2(square)]
    all_to_all x1, waiting for transfers between devices: 4.24 us -> 5.19 us  [shards(): parts = lax.all_to_all(payload, 'seq', 0, 0, tiled=True)]
  transfers between devices with their start and end apart: 13 -> 13, of which waited for: 8 -> 10; matrix products, arithmetic and copies ran while one was open for 1% -> 0% of each run, Pallas kernels for 37% -> 36%
where the time goes in v2:
time: 84.8 us; the launch traced here: 84.5 us
  Pallas kernels  43 us (51%)
  starting transfers between devices  29.1 us (34%)
  waiting for transfers between devices  11.4 us (13%)
    all_to_all x1, starting transfers between devices, shards(): parts = lax.all_to_all(payload, 'seq', 0, 0, tiled=True)  11 us
    pallas_call x1, Pallas kernels, chain_call(): pl.pallas_call(chain_kernel, out_shape=(far_out((TOK, STATE), F32), far_o...  9.73 us
    pallas_call x1, Pallas kernels, within_call(): pl.pallas_call(within_kernel, out_shape=(far_out((TOK, WIDTH), BF16), far...  9.02 us
    pallas_call x1, Pallas kernels, prepare_call(): pl.pallas_call(prepare_kernel, out_shape=(far_out((2 * PAD, TOK), F32), f...  7.02 us
    all_to_all x1, waiting for transfers between devices, shards(): parts = lax.all_to_all(payload, 'seq', 0, 0, tiled=True)  5.19 us
    pallas_call x1, Pallas kernels, input_call(): pl.pallas_call(input_kernel, out_shape=jax.ShapeDtypeStruct((TOK, WIDTH),...  4.92 us
    ppermute x3, starting transfers between devices, shards(): mine = [own] + [lax.ppermute(own, 'head', along_y(k)) for k in (1, 2, 3)]  4.68 us
    all_to_all x1, starting transfers between devices, shards(): lax.all_to_all(entering, 'seq', 0, 0, tiled=True).reshape(2 * STATE, WIDTH)  4.63 us
  transfers between devices with their start and end apart: 13, of which 10 were waited for; matrix products, arithmetic and copies ran while one was open for 0% of the time, Pallas kernels for 36%

profile of v2, /device:TPU:1, one launch (start us, length us, event | category | flops | bytes accessed | tf_op | source)
XLA Modules:
  0.0 84.5 jit_solution(5505244609791531964)
XLA Ops:
  0.6 0.9 %join.1.m0 = bf16[256,256]{1,0:T(8,128)(2,1)S(1)} custom-call(bf16[256,128]{1,0:T(8,128)(2,1)} %a_hbm.1, bf16[256,128]{1,0:T(8,128)(2,1)} %b_hbm.1), custom_call_target="tpu_custom_call" | custom-call | tf_op jit(solution)/shard_map/join/pallas_call | solution.py:604
  1.5 3.6 %collective-permute-start.2 = (bf16[256,256]{1,0:T(8,128)(2,1)S(1)}, bf16[256,256]{1,0:T(8,128)(2,1)S(1)}, u32[]{:S(2)}, u32[]{:S(2)}) collective-permute-start(bf16[256,256]{1,0:T(8,128)(2,1)S(1)} %join.1.m0), channel_id=1, source_target_pairs={{0,6},{1,7},{2,0},{3,1},{4,2},{5,3},{6,4},{7,5},{8,14},{9,15},{10,... | collective-permute-start | bytes 393224 | tf_op jit(solution)/shard_map/ppermute | solution.py:663
  5.2 0.3 collective-permute-start.1
  5.5 0.7 collective-permute-start
  6.2 7.0 %prepare.1 = (f32[32,2048]{1,0:T(8,128)}, bf16[2048,128]{1,0:T(8,128)(2,1)}, bf16[128,128]{1,0:T(8,128)(2,1)}, bf16[2048,640]{1,0:T(8,128)(2,1)S(1)}, bf16[2048,...) custom-call(s32[1,4]{1,0:T(1,128)} %off_hbm.3, f32[10,2048]{1,0:T(8,128)} %l_hbm.1, bf16[128,256]{1,0:T(8,128)(2,1)} %constant.22.clone.sums_hbm, ...), custom_call_target="tpu_custom_call" | custom-call | flops 4000000000 | bytes 16000000 | tf_op jit(solution)/shard_map/prepare/pallas_call | solution.py:199
  13.3 1.5 %collective-permute-done.m1 = bf16[256,256]{1,0:T(8,128)(2,1)S(1)} collective-permute-done((bf16[256,256]{1,0:T(8,128)(2,1)S(1)}, bf16[256,256]{1,0:T(8,128)(2,1)S(1)}, u32[]{:S(2)}, u32[]{:S(2)}) %collective-permute-start) | collective-permute-done | bytes 131104 | tf_op jit(solution)/shard_map/ppermute | solution.py:663
  14.8 0.6 collective-permute-start.3
  15.4 0.5 collective-permute-start.5
  16.0 0.4 collective-permute-done.3.o0
  16.4 0.4 collective-permute-done.4.o1
  16.7 0.3 collective-permute-done.5.o2
  17.0 0.4 collective-permute-done.6.o3
  17.4 4.6 %states.1 = (bf16[32,8,768]{2,1,0:T(8,128)(2,1)}, bf16[2048,256]{1,0:T(8,128)(2,1)}) custom-call(s32[2]{0:T(128)S(1)} %pad_add_fusion.place, bf16[256,256]{1,0:T(8,128)(2,1)S(1)} %join.1.m0, bf16[256,256]{1,0:T(8,128)(2,1)S(1)} %collective-permute-done.m1, bf16[256,256]{1,0:T(8,128)(2,1)S(1)} %collective-permute-done.1.m2, ...), custom_call_target="tpu_custom_call" | custom-call | flops 700000000 | bytes 6500000 | tf_op jit(solution)/shard_map/states/pallas_call | solution.py:269
  22.0 11.0 %all-to-all-start = ((bf16[32,8,768]{2,1,0:T(8,128)(2,1)}), bf16[32,8,768]{2,1,0:T(8,128)(2,1)S(1)}, u32[]{:S(2)}, u32[]{:S(2)}) async-start(bf16[32,8,768]{2,1,0:T(8,128)(2,1)} %get-tuple-element.43), calls=%async_computation | async-start | bytes 786432 | tf_op jit(solution)/shard_map/all_to_all | solution.py:670
  33.1 0.1 broadcast_in_dim_reshape.3.skip_ref
  33.2 9.0 %within_chunks.1 = (bf16[2048,640]{1,0:T(8,128)(2,1)}, bf16[2048,128]{1,0:T(8,128)(2,1)}) custom-call(s32[1,4]{1,0:T(1,128)} %off_hbm.3, bf16[2048,640]{1,0:T(8,128)(2,1)} %x_hbm.5, bf16[2048,640]{1,0:T(8,128)(2,1)} %g_hbm.5, bf16[2048,256]{1,0:T(8,128)(2,1)} %get-tuple-element.44.bc_hbm, f32[32,2048]{1,0:T(8,128)} %get-tuple-element.45.cum_hbm, ...), custom_call_target="tpu_custom_call" | custom-call | flops 4000000000 | bytes 16000000 | tf_op jit(solution)/shard_map/within_chunks/pallas_call | solution.py:382
  42.3 5.2 %all-to-all-done.in_ref = bf16[32,8,768]{2,1,0:T(8,128)(2,1)S(1)} async-done(((bf16[32,8,768]{2,1,0:T(8,128)(2,1)}), bf16[32,8,768]{2,1,0:T(8,128)(2,1)S(1)}, u32[]{:S(2)}, u32[]{:S(2)}) %all-to-all-start) | async-done | bytes 393248 | tf_op jit(solution)/shard_map/all_to_all | solution.py:670
  47.5 1.1 %scan.1 = bf16[32,8,640]{2,1,0:T(8,128)(2,1)} custom-call(s32[1]{0:T(128)} %bitcast.2.me, bf16[32,8,768]{2,1,0:T(8,128)(2,1)S(1)} %all-to-all-done.in_ref, bf16[128,640]{1,0:T(8,128)(2,1)S(1)} %copy-done), custom_call_target="tpu_custom_call" | custom-call | tf_op jit(solution)/shard_map/scan/pallas_call | solution.py:306
  48.6 4.6 %all-to-all-start.1 = ((bf16[32,8,640]{2,1,0:T(8,128)(2,1)}), bf16[32,8,640]{2,1,0:T(8,128)(2,1)S(1)}, u32[]{:S(2)}, u32[]{:S(2)}) async-start(bf16[32,8,640]{2,1,0:T(8,128)(2,1)} %scan.1), calls=%async_computation.1 | async-start | bytes 655360 | tf_op jit(solution)/shard_map/all_to_all | solution.py:675
  53.2 9.7 %chunk_chain.1 = (f32[2048,128]{1,0:T(8,128)}, f32[2048,128]{1,0:T(8,128)}, bf16[16,128,640]{2,1,0:T(8,128)(2,1)}, bf16[2048,640]{1,0:T(8,128)(2,1)S(1)}) custom-call(bf16[2048,640]{1,0:T(8,128)(2,1)} %x_hbm.5, bf16[2048,640]{1,0:T(8,128)(2,1)} %g_hbm.5, bf16[2048,256]{1,0:T(8,128)(2,1)} %get-tuple-element.44.bc_hbm, ...), custom_call_target="tpu_custom_call" | custom-call | flops 4000000000 | bytes 16000000 | tf_op jit(solution)/shard_map/chunk_chain/pallas_call | solution.py:468
  63.0 1.3 %all-to-all-done.1 = bf16[32,8,640]{2,1,0:T(8,128)(2,1)S(1)} async-done(((bf16[32,8,640]{2,1,0:T(8,128)(2,1)}), bf16[32,8,640]{2,1,0:T(8,128)(2,1)S(1)}, u32[]{:S(2)}, u32[]{:S(2)}) %all-to-all-start.1) | async-done | bytes 327712 | tf_op jit(solution)/shard_map/all_to_all | solution.py:675
  64.2 4.3 %carry.1 = (f32[4,256,256]{2,1,0:T(8,128)S(1)}, bf16[4,256,256]{2,1,0:T(8,128)(2,1)S(1)}) custom-call(s32[2]{0:T(128)S(1)} %pad_add_fusion.place, bf16[2048,640]{1,0:T(8,128)(2,1)S(1)} %get-tuple-element.54.xt_ref, bf16[2048,640]{1,0:T(8,128)(2,1)} %get-tuple-element.41.ge_hbm, f32[2048,128]{1,0:T(8,128)} %get-tuple-element.55.gb_hbm, ...), custom_call_target="tpu_custom_call" | custom-call | flops 700000000 | bytes 9000000 | tf_op jit(solution)/shard_map/carry/pallas_call | solution.py:524
  68.5 3.9 %collective-permute-start.7 = (bf16[4,256,256]{2,1,0:T(8,128)(2,1)S(1)}, bf16[4,256,256]{2,1,0:T(8,128)(2,1)S(1)}, u32[]{:S(2)}, u32[]{:S(2)}) collective-permute-start(bf16[4,256,256]{2,1,0:T(8,128)(2,1)S(1)} %get-tuple-element.58), channel_id=1, source_target_pairs={{0,1},{1,0},{2,3},{3,2},{4,5},{5,4},{6,7},{7,6},{8,9},{9,8},{10,11... | collective-permute-start | bytes 1572872 | tf_op jit(solution)/shard_map/ppermute | solution.py:680
  72.4 1.5 %collective-permute-done.7.got_ref = bf16[4,256,256]{2,1,0:T(8,128)(2,1)S(1)} collective-permute-done((bf16[4,256,256]{2,1,0:T(8,128)(2,1)S(1)}, bf16[4,256,256]{2,1,0:T(8,128)(2,1)S(1)}, u32[]{:S(2)}, u32[]{:S(2)}) %collective-permute-start.7) | collective-permute-done | bytes 524320 | tf_op jit(solution)/shard_map/ppermute | solution.py:680
  74.0 0.7 pair_sums.1
  74.6 1.2 %collective-permute-start.8 = (bf16[256,256]{1,0:T(8,128)(2,1)S(1)}, bf16[256,256]{1,0:T(8,128)(2,1)S(1)}, u32[]{:S(2)}, u32[]{:S(2)}) collective-permute-start(bf16[256,256]{1,0:T(8,128)(2,1)S(1)} %get-tuple-element.60), channel_id=1, source_target_pairs={{0,2},{1,3},{2,4},{3,5},{4,6},{5,7},{6,0},{7,1},{8,10},{9,11},{10,... | collective-permute-start | bytes 393224 | tf_op jit(solution)/shard_map/ppermute | solution.py:681
  75.8 1.6 %collective-permute-start.9 = (bf16[256,256]{1,0:T(8,128)(2,1)S(1)}, bf16[256,256]{1,0:T(8,128)(2,1)S(1)}, u32[]{:S(2)}, u32[]{:S(2)}) collective-permute-start(bf16[256,256]{1,0:T(8,128)(2,1)S(1)} %get-tuple-element.61), channel_id=1, source_target_pairs={{0,4},{1,5},{2,6},{3,7},{4,0},{5,1},{6,2},{7,3},{8,12},{9,13},{10,... | collective-permute-start | bytes 393224 | tf_op jit(solution)/shard_map/ppermute | solution.py:681
  77.4 0.9 %collective-permute-start.10 = (bf16[256,256]{1,0:T(8,128)(2,1)S(1)}, bf16[256,256]{1,0:T(8,128)(2,1)S(1)}, u32[]{:S(2)}, u32[]{:S(2)}) collective-permute-start(bf16[256,256]{1,0:T(8,128)(2,1)S(1)} %get-tuple-element.62), channel_id=1, source_target_pairs={{0,6},{1,7},{2,0},{3,1},{4,2},{5,3},{6,4},{7,5},{8,14},{9,15},{10,... | collective-permute-start | bytes 393224 | tf_op jit(solution)/shard_map/ppermute | solution.py:681
  78.3 4.9 %input_gradient.1 = bf16[2048,640]{1,0:T(8,128)(2,1)} custom-call(bf16[2048,640]{1,0:T(8,128)(2,1)} %get-tuple-element.48.gx_hbm, bf16[16,128,640]{2,1,0:T(8,128)(2,1)} %get-tuple-element.52.tst_hbm, bf16[2048,256]{1,0:T(8,128)(2,1)} %get-tuple-element.44.bc_hbm, bf16[2048,128]{1,0:T(8,128)(2,1)} %get-tuple-element.49.sc_hbm, bf16[256,640]{1,0:T(8,128)(2,1)S(1)} %bitcast.5, ...), custom_call_target="tpu_custom_call" | custom-call | flops 2000000000 | bytes 12000000 | tf_op jit(solution)/shard_map/input_gradient/pallas_call | solution.py:572
  83.2 0.2 collective-permute-done.9.c_ref
  83.4 0.3 collective-permute-done.10.d_ref
  83.7 0.7 totals.1
  (15 shorter events, 0.2 us)
Async XLA Ops:
  1.5 11.7 %collective-permute-start.2 = (bf16[256,256]{1,0:T(8,128)(2,1)S(1)}, bf16[256,256]{1,0:T(8,128)(2,1)S(1)}, u32[]{:S(2)}, u32[]{:S(2)}) collective-permute-start(bf16[256,256]{1,0:T(8,128)(2,1)S(1)} %join.1.m0), channel_id=1, source_target_pairs={{0,6},{1,7},{2,0},{3,1},{4,2},{5,3},{6,4},{7,5},{8,14},{9,15},{10,... | collective-permute-start | bytes 393224 | tf_op jit(solution)/shard_map/ppermute | solution.py:663
  5.2 8.1 %collective-permute-start.1 = (bf16[256,256]{1,0:T(8,128)(2,1)S(1)}, bf16[256,256]{1,0:T(8,128)(2,1)S(1)}, u32[]{:S(2)}, u32[]{:S(2)}) collective-permute-start(bf16[256,256]{1,0:T(8,128)(2,1)S(1)} %join.1.m0), channel_id=1, source_target_pairs={{0,4},{1,5},{2,6},{3,7},{4,0},{5,1},{6,2},{7,3},{8,12},{9,13},{10,... | collective-permute-start | bytes 393224 | tf_op jit(solution)/shard_map/ppermute | solution.py:663
  5.5 9.3 %collective-permute-start = (bf16[256,256]{1,0:T(8,128)(2,1)S(1)}, bf16[256,256]{1,0:T(8,128)(2,1)S(1)}, u32[]{:S(2)}, u32[]{:S(2)}) collective-permute-start(bf16[256,256]{1,0:T(8,128)(2,1)S(1)} %join.1.m0), channel_id=1, source_target_pairs={{0,2},{1,3},{2,4},{3,5},{4,6},{5,7},{6,0},{7,1},{8,10},{9,11},{10,... | collective-permute-start | bytes 393224 | tf_op jit(solution)/shard_map/ppermute | solution.py:663
  14.8 1.6 %collective-permute-start.3 = (bf16[256,256]{1,0:T(8,128)(2,1)S(1)}, bf16[256,256]{1,0:T(8,128)(2,1)S(1)}, u32[]{:S(2)}, u32[]{:S(2)}) collective-permute-start(bf16[256,256]{1,0:T(8,128)(2,1)S(1)} %join.1.m0), channel_id=1, source_target_pairs={{0,1},{1,0},{2,3},{3,2},{4,5},{5,4},{6,7},{7,6},{8,9},{9,8},{10,11... | collective-permute-start | bytes 393224 | tf_op jit(solution)/shard_map/ppermute | solution.py:668
  15.4 1.3 %collective-permute-start.4 = (bf16[256,256]{1,0:T(8,128)(2,1)S(1)}, bf16[256,256]{1,0:T(8,128)(2,1)S(1)}, u32[]{:S(2)}, u32[]{:S(2)}) collective-permute-start(bf16[256,256]{1,0:T(8,128)(2,1)S(1)} %collective-permute-done.m1), channel_id=1, source_target_pairs={{0,1},{1,0},{2,3},{3,2},{4,5},{5,4},{6,7},{7,6},{8,9},{9,8},{10,11... | collective-permute-start | bytes 393224 | tf_op jit(solution)/shard_map/ppermute | solution.py:668
  15.4 1.6 %collective-permute-start.5 = (bf16[256,256]{1,0:T(8,128)(2,1)S(1)}, bf16[256,256]{1,0:T(8,128)(2,1)S(1)}, u32[]{:S(2)}, u32[]{:S(2)}) collective-permute-start(bf16[256,256]{1,0:T(8,128)(2,1)S(1)} %collective-permute-done.1.m2), channel_id=1, source_target_pairs={{0,1},{1,0},{2,3},{3,2},{4,5},{5,4},{6,7},{7,6},{8,9},{9,8},{10,11... | collective-permute-start | bytes 393224 | tf_op jit(solution)/shard_map/ppermute | solution.py:668
  15.9 1.5 %collective-permute-start.6 = (bf16[256,256]{1,0:T(8,128)(2,1)S(1)}, bf16[256,256]{1,0:T(8,128)(2,1)}, u32[]{:S(2)}, u32[]{:S(2)}) collective-permute-start(bf16[256,256]{1,0:T(8,128)(2,1)S(1)} %collective-permute-done.2.m3), channel_id=1, source_target_pairs={{0,1},{1,0},{2,3},{3,2},{4,5},{5,4},{6,7},{7,6},{8,9},{9,8},{10,11... | collective-permute-start | bytes 393224 | tf_op jit(solution)/shard_map/ppermute | solution.py:668
  17.4 15.7 %copy-start.3 = (f32[10]{0:T(128)S(1)}, f32[10]{0:T(128)}, u32[]{:S(2)}) copy-start(f32[10]{0:T(128)} %param.15) | copy-start | bytes 124
  22.0 25.5 %all-to-all-start = ((bf16[32,8,768]{2,1,0:T(8,128)(2,1)}), bf16[32,8,768]{2,1,0:T(8,128)(2,1)S(1)}, u32[]{:S(2)}, u32[]{:S(2)}) async-start(bf16[32,8,768]{2,1,0:T(8,128)(2,1)} %get-tuple-element.43), calls=%async_computation | async-start | bytes 786432 | tf_op jit(solution)/shard_map/all_to_all | solution.py:670
  33.2 14.2 %copy-start = (bf16[128,640]{1,0:T(8,128)(2,1)S(1)}, bf16[128,640]{1,0:T(8,128)(2,1)}, u32[]{:S(2)}) copy-start(bf16[128,640]{1,0:T(8,128)(2,1)} %constant.21.clone.spf_ref.sp_ref) | copy-start | bytes 491524
  33.2 20.0 %copy-start.1 = (bf16[128,1280]{1,0:T(8,128)(2,1)S(1)}, bf16[128,1280]{1,0:T(8,128)(2,1)}, u32[]{:S(2)}) copy-start(bf16[128,1280]{1,0:T(8,128)(2,1)} %constant.20.clone.sp_ref) | copy-start | bytes 983044
  33.2 20.0 %copy-start.2 = (bf16[128,128]{1,0:T(8,128)(2,1)S(1)}, bf16[128,128]{1,0:T(8,128)(2,1)}, u32[]{:S(2)}) copy-start(bf16[128,128]{1,0:T(8,128)(2,1)} %get-tuple-element.42.dec_hbm.dec_ref) | copy-start | bytes 98308
  48.6 15.7 %all-to-all-start.1 = ((bf16[32,8,640]{2,1,0:T(8,128)(2,1)}), bf16[32,8,640]{2,1,0:T(8,128)(2,1)S(1)}, u32[]{:S(2)}, u32[]{:S(2)}) async-start(bf16[32,8,640]{2,1,0:T(8,128)(2,1)} %scan.1), calls=%async_computation.1 | async-start | bytes 655360 | tf_op jit(solution)/shard_map/all_to_all | solution.py:675
  68.5 5.5 %collective-permute-start.7 = (bf16[4,256,256]{2,1,0:T(8,128)(2,1)S(1)}, bf16[4,256,256]{2,1,0:T(8,128)(2,1)S(1)}, u32[]{:S(2)}, u32[]{:S(2)}) collective-permute-start(bf16[4,256,256]{2,1,0:T(8,128)(2,1)S(1)} %get-tuple-element.58), channel_id=1, source_target_pairs={{0,1},{1,0},{2,3},{3,2},{4,5},{5,4},{6,7},{7,6},{8,9},{9,8},{10,11... | collective-permute-start | bytes 1572872 | tf_op jit(solution)/shard_map/ppermute | solution.py:680
  74.6 8.6 %collective-permute-start.8 = (bf16[256,256]{1,0:T(8,128)(2,1)S(1)}, bf16[256,256]{1,0:T(8,128)(2,1)S(1)}, u32[]{:S(2)}, u32[]{:S(2)}) collective-permute-start(bf16[256,256]{1,0:T(8,128)(2,1)S(1)} %get-tuple-element.60), channel_id=1, source_target_pairs={{0,2},{1,3},{2,4},{3,5},{4,6},{5,7},{6,0},{7,1},{8,10},{9,11},{10,... | collective-permute-start | bytes 393224 | tf_op jit(solution)/shard_map/ppermute | solution.py:681
  75.8 7.6 %collective-permute-start.9 = (bf16[256,256]{1,0:T(8,128)(2,1)S(1)}, bf16[256,256]{1,0:T(8,128)(2,1)S(1)}, u32[]{:S(2)}, u32[]{:S(2)}) collective-permute-start(bf16[256,256]{1,0:T(8,128)(2,1)S(1)} %get-tuple-element.61), channel_id=1, source_target_pairs={{0,4},{1,5},{2,6},{3,7},{4,0},{5,1},{6,2},{7,3},{8,12},{9,13},{10,... | collective-permute-start | bytes 393224 | tf_op jit(solution)/shard_map/ppermute | solution.py:681
  77.4 6.3 %collective-permute-start.10 = (bf16[256,256]{1,0:T(8,128)(2,1)S(1)}, bf16[256,256]{1,0:T(8,128)(2,1)S(1)}, u32[]{:S(2)}, u32[]{:S(2)}) collective-permute-start(bf16[256,256]{1,0:T(8,128)(2,1)S(1)} %get-tuple-element.62), channel_id=1, source_target_pairs={{0,6},{1,7},{2,0},{3,1},{4,2},{5,3},{6,4},{7,5},{8,14},{9,15},{10,... | collective-permute-start | bytes 393224 | tf_op jit(solution)/shard_map/ppermute | solution.py:681

commit v3 on v2

--- a/solution.py
+++ b/solution.py
@@ -435,7 +435,7 @@
             r = pl.ds(pl.multiple_of(c * Q, Q), Q)
             state = s_ref[...]
             b = bc_ref[r, :STATE]
-            gc_ref[r, :] = tn(z_ref[r, :], b) + nt(g_ref[r, :], state.astype(BF16))
+            gc_ref[r, :] = (tn(z_ref[r, :], b) + nt(g_ref[r, :], state.astype(BF16))).astype(BF16)
             s_ref[...] = d_ref[pl.ds(c, 1), :] * state + tn(b, x_ref[r, :])
             c = back * per + per - 1 - sub
             r = pl.ds(pl.multiple_of(c * Q, Q), Q)
@@ -443,7 +443,7 @@
             low = state.astype(BF16)
             tst_ref[c] = low
             q = bc_ref[r, STATE:]
-            gb_ref[r, :] = nn(z_ref[r, :], q) + nt(x_ref[r, :], low)
+            gb_ref[r, :] = (nn(z_ref[r, :], q) + nt(x_ref[r, :], low)).astype(BF16)
             t_ref[...] = d_ref[pl.ds(c, 1), :] * state + tn(q, g_ref[r, :])
         block_copy(gc_ref, gc_hbm, out_sem, 0, step).start()
         block_copy(gb_ref, gb_hbm, out_sem, 1, back).start()
@@ -468,8 +468,8 @@
     return pl.pallas_call(
         chain_kernel,
         out_shape=(
-            far_out((TOK, STATE), F32),
-            far_out((TOK, STATE), F32),
+            far_out((TOK, STATE), BF16),
+            far_out((TOK, STATE), BF16),
             far_out((CHUNKS, STATE, WIDTH), BF16),
             kept((TOK, WIDTH), BF16),
         ),
@@ -481,8 +481,8 @@
             pltpu.VMEM((TOK, 2 * STATE), BF16),
             pltpu.VMEM((TOK, STATE), BF16),
             pltpu.VMEM((TOK, STATE), BF16),
-            pltpu.VMEM((TOK, STATE), F32),
-            pltpu.VMEM((TOK, STATE), F32),
+            pltpu.VMEM((TOK, STATE), BF16),
+            pltpu.VMEM((TOK, STATE), BF16),
             pltpu.VMEM((CHUNKS, STATE, WIDTH), BF16),
             pltpu.VMEM((STATE, WIDTH), F32),
             pltpu.VMEM((STATE, WIDTH), F32),
@@ -531,8 +531,8 @@
         out_specs=(WHOLE, WHOLE),
         scratch_shapes=[
             pltpu.VMEM((TOK, WIDTH), BF16),
-            pltpu.VMEM((TOK, STATE), F32),
-            pltpu.VMEM((TOK, STATE), F32),
+            pltpu.VMEM((TOK, STATE), BF16),
+            pltpu.VMEM((TOK, STATE), BF16),
             pltpu.SemaphoreType.DMA((3, 4)),
         ],
         compiler_params=options(),

time: 84.8 us -> 84.8 us (level)
  no operation moved by 1% of the time
where the time goes in v3:
time: 84.8 us; the launch traced here: 84.4 us
  Pallas kernels  42.9 us (51%)
  starting transfers between devices  29.1 us (34%)
  waiting for transfers between devices  11.4 us (13%)
    all_to_all x1, starting transfers between devices, shards(): parts = lax.all_to_all(payload, 'seq', 0, 0, tiled=True)  11 us
    pallas_call x1, Pallas kernels, chain_call(): pl.pallas_call(chain_kernel, out_shape=(far_out((TOK, STATE), BF16), far_...  9.73 us
    pallas_call x1, Pallas kernels, within_call(): pl.pallas_call(within_kernel, out_shape=(far_out((TOK, WIDTH), BF16), far...  9.04 us
    pallas_call x1, Pallas kernels, prepare_call(): pl.pallas_call(prepare_kernel, out_shape=(far_out((2 * PAD, TOK), F32), f...  7.02 us
    all_to_all x1, waiting for transfers between devices, shards(): parts = lax.all_to_all(payload, 'seq', 0, 0, tiled=True)  5.18 us
    pallas_call x1, Pallas kernels, input_call(): pl.pallas_call(input_kernel, out_shape=jax.ShapeDtypeStruct((TOK, WIDTH),...  4.92 us
    ppermute x3, starting transfers between devices, shards(): mine = [own] + [lax.ppermute(own, 'head', along_y(k)) for k in (1, 2, 3)]  4.68 us
    all_to_all x1, starting transfers between devices, shards(): lax.all_to_all(entering, 'seq', 0, 0, tiled=True).reshape(2 * STATE, WIDTH)  4.63 us
  transfers between devices with their start and end apart: 13, of which 10 were waited for; matrix products, arithmetic and copies ran while one was open for 0% of the time, Pallas kernels for 36%

profile of v3, /device:TPU:1, one launch (start us, length us, event | category | flops | bytes accessed | tf_op | source)
XLA Modules:
  0.0 84.4 jit_solution(5292302825355925288)
XLA Ops:
  0.6 0.9 %join.1.m0 = bf16[256,256]{1,0:T(8,128)(2,1)S(1)} custom-call(bf16[256,128]{1,0:T(8,128)(2,1)} %a_hbm.1, bf16[256,128]{1,0:T(8,128)(2,1)} %b_hbm.1), custom_call_target="tpu_custom_call" | custom-call | tf_op jit(solution)/shard_map/join/pallas_call | solution.py:604
  1.5 3.6 %collective-permute-start.2 = (bf16[256,256]{1,0:T(8,128)(2,1)S(1)}, bf16[256,256]{1,0:T(8,128)(2,1)S(1)}, u32[]{:S(2)}, u32[]{:S(2)}) collective-permute-start(bf16[256,256]{1,0:T(8,128)(2,1)S(1)} %join.1.m0), channel_id=1, source_target_pairs={{0,6},{1,7},{2,0},{3,1},{4,2},{5,3},{6,4},{7,5},{8,14},{9,15},{10,... | collective-permute-start | bytes 393224 | tf_op jit(solution)/shard_map/ppermute | solution.py:663
  5.2 0.3 collective-permute-start.1
  5.5 0.7 collective-permute-start
  6.2 7.0 %prepare.1 = (f32[32,2048]{1,0:T(8,128)}, bf16[2048,128]{1,0:T(8,128)(2,1)}, bf16[128,128]{1,0:T(8,128)(2,1)}, bf16[2048,640]{1,0:T(8,128)(2,1)S(1)}, bf16[2048,...) custom-call(s32[1,4]{1,0:T(1,128)} %off_hbm.3, f32[10,2048]{1,0:T(8,128)} %l_hbm.1, bf16[128,256]{1,0:T(8,128)(2,1)} %constant.22.clone.sums_hbm, ...), custom_call_target="tpu_custom_call" | custom-call | flops 4000000000 | bytes 16000000 | tf_op jit(solution)/shard_map/prepare/pallas_call | solution.py:199
  13.3 1.5 %collective-permute-done.m1 = bf16[256,256]{1,0:T(8,128)(2,1)S(1)} collective-permute-done((bf16[256,256]{1,0:T(8,128)(2,1)S(1)}, bf16[256,256]{1,0:T(8,128)(2,1)S(1)}, u32[]{:S(2)}, u32[]{:S(2)}) %collective-permute-start) | collective-permute-done | bytes 131104 | tf_op jit(solution)/shard_map/ppermute | solution.py:663
  14.8 0.6 collective-permute-start.3
  15.4 0.5 collective-permute-start.5
  16.0 0.4 collective-permute-done.3.o0
  16.4 0.4 collective-permute-done.4.o1
  16.7 0.3 collective-permute-done.5.o2
  17.0 0.4 collective-permute-done.6.o3
  17.4 4.6 %states.1 = (bf16[32,8,768]{2,1,0:T(8,128)(2,1)}, bf16[2048,256]{1,0:T(8,128)(2,1)}) custom-call(s32[2]{0:T(128)S(1)} %pad_add_fusion.place, bf16[256,256]{1,0:T(8,128)(2,1)S(1)} %join.1.m0, bf16[256,256]{1,0:T(8,128)(2,1)S(1)} %collective-permute-done.m1, bf16[256,256]{1,0:T(8,128)(2,1)S(1)} %collective-permute-done.1.m2, ...), custom_call_target="tpu_custom_call" | custom-call | flops 700000000 | bytes 6500000 | tf_op jit(solution)/shard_map/states/pallas_call | solution.py:269
  22.0 11.0 %all-to-all-start = ((bf16[32,8,768]{2,1,0:T(8,128)(2,1)}), bf16[32,8,768]{2,1,0:T(8,128)(2,1)S(1)}, u32[]{:S(2)}, u32[]{:S(2)}) async-start(bf16[32,8,768]{2,1,0:T(8,128)(2,1)} %get-tuple-element.43), calls=%async_computation | async-start | bytes 786432 | tf_op jit(solution)/shard_map/all_to_all | solution.py:670
  33.1 0.1 broadcast_in_dim_reshape.3.skip_ref
  33.2 9.0 %within_chunks.1 = (bf16[2048,640]{1,0:T(8,128)(2,1)}, bf16[2048,128]{1,0:T(8,128)(2,1)}) custom-call(s32[1,4]{1,0:T(1,128)} %off_hbm.3, bf16[2048,640]{1,0:T(8,128)(2,1)} %x_hbm.5, bf16[2048,640]{1,0:T(8,128)(2,1)} %g_hbm.5, bf16[2048,256]{1,0:T(8,128)(2,1)} %get-tuple-element.44.bc_hbm, f32[32,2048]{1,0:T(8,128)} %get-tuple-element.45.cum_hbm, ...), custom_call_target="tpu_custom_call" | custom-call | flops 4000000000 | bytes 16000000 | tf_op jit(solution)/shard_map/within_chunks/pallas_call | solution.py:382
  42.3 5.2 %all-to-all-done.in_ref = bf16[32,8,768]{2,1,0:T(8,128)(2,1)S(1)} async-done(((bf16[32,8,768]{2,1,0:T(8,128)(2,1)}), bf16[32,8,768]{2,1,0:T(8,128)(2,1)S(1)}, u32[]{:S(2)}, u32[]{:S(2)}) %all-to-all-start) | async-done | bytes 393248 | tf_op jit(solution)/shard_map/all_to_all | solution.py:670
  47.4 1.1 %scan.1 = bf16[32,8,640]{2,1,0:T(8,128)(2,1)} custom-call(s32[1]{0:T(128)} %bitcast.2.me, bf16[32,8,768]{2,1,0:T(8,128)(2,1)S(1)} %all-to-all-done.in_ref, bf16[128,640]{1,0:T(8,128)(2,1)S(1)} %copy-done), custom_call_target="tpu_custom_call" | custom-call | tf_op jit(solution)/shard_map/scan/pallas_call | solution.py:306
  48.5 4.6 %all-to-all-start.1 = ((bf16[32,8,640]{2,1,0:T(8,128)(2,1)}), bf16[32,8,640]{2,1,0:T(8,128)(2,1)S(1)}, u32[]{:S(2)}, u32[]{:S(2)}) async-start(bf16[32,8,640]{2,1,0:T(8,128)(2,1)} %scan.1), calls=%async_computation.1 | async-start | bytes 655360 | tf_op jit(solution)/shard_map/all_to_all | solution.py:675
  53.2 9.7 %chunk_chain.1 = (bf16[2048,128]{1,0:T(8,128)(2,1)}, bf16[2048,128]{1,0:T(8,128)(2,1)}, bf16[16,128,640]{2,1,0:T(8,128)(2,1)}, bf16[2048,640]{1,0:T(8,128)(2,1)S(1)}) custom-call(bf16[2048,640]{1,0:T(8,128)(2,1)} %x_hbm.5, bf16[2048,640]{1,0:T(8,128)(2,1)} %g_hbm.5, bf16[2048,256]{1,0:T(8,128)(2,1)} %get-tuple-element.44.bc_hbm, ...), custom_call_target="tpu_custom_call" | custom-call | flops 4000000000 | bytes 16000000 | tf_op jit(solution)/shard_map/chunk_chain/pallas_call | solution.py:468
  62.9 1.3 %all-to-all-done.1 = bf16[32,8,640]{2,1,0:T(8,128)(2,1)S(1)} async-done(((bf16[32,8,640]{2,1,0:T(8,128)(2,1)}), bf16[32,8,640]{2,1,0:T(8,128)(2,1)S(1)}, u32[]{:S(2)}, u32[]{:S(2)}) %all-to-all-start.1) | async-done | bytes 327712 | tf_op jit(solution)/shard_map/all_to_all | solution.py:675
  64.2 4.2 %carry.1 = (f32[4,256,256]{2,1,0:T(8,128)S(1)}, bf16[4,256,256]{2,1,0:T(8,128)(2,1)S(1)}) custom-call(s32[2]{0:T(128)S(1)} %pad_add_fusion.place, bf16[2048,640]{1,0:T(8,128)(2,1)S(1)} %get-tuple-element.54.xt_ref, bf16[2048,640]{1,0:T(8,128)(2,1)} %get-tuple-element.41.ge_hbm, bf16[2048,128]{1,0:T(8,128)(2,1)} %get-tuple-element.55.gb_hbm, ...), custom_call_target="tpu_custom_call" | custom-call | flops 700000000 | bytes 9000000 | tf_op jit(solution)/shard_map/carry/pallas_call | solution.py:524
  68.5 3.9 %collective-permute-start.7 = (bf16[4,256,256]{2,1,0:T(8,128)(2,1)S(1)}, bf16[4,256,256]{2,1,0:T(8,128)(2,1)S(1)}, u32[]{:S(2)}, u32[]{:S(2)}) collective-permute-start(bf16[4,256,256]{2,1,0:T(8,128)(2,1)S(1)} %get-tuple-element.58), channel_id=1, source_target_pairs={{0,1},{1,0},{2,3},{3,2},{4,5},{5,4},{6,7},{7,6},{8,9},{9,8},{10,11... | collective-permute-start | bytes 1572872 | tf_op jit(solution)/shard_map/ppermute | solution.py:680
  72.4 1.5 %collective-permute-done.7.got_ref = bf16[4,256,256]{2,1,0:T(8,128)(2,1)S(1)} collective-permute-done((bf16[4,256,256]{2,1,0:T(8,128)(2,1)S(1)}, bf16[4,256,256]{2,1,0:T(8,128)(2,1)S(1)}, u32[]{:S(2)}, u32[]{:S(2)}) %collective-permute-start.7) | collective-permute-done | bytes 524320 | tf_op jit(solution)/shard_map/ppermute | solution.py:680
  73.9 0.7 pair_sums.1
  74.6 1.2 %collective-permute-start.8 = (bf16[256,256]{1,0:T(8,128)(2,1)S(1)}, bf16[256,256]{1,0:T(8,128)(2,1)S(1)}, u32[]{:S(2)}, u32[]{:S(2)}) collective-permute-start(bf16[256,256]{1,0:T(8,128)(2,1)S(1)} %get-tuple-element.60), channel_id=1, source_target_pairs={{0,2},{1,3},{2,4},{3,5},{4,6},{5,7},{6,0},{7,1},{8,10},{9,11},{10,... | collective-permute-start | bytes 393224 | tf_op jit(solution)/shard_map/ppermute | solution.py:681
  75.7 1.6 %collective-permute-start.9 = (bf16[256,256]{1,0:T(8,128)(2,1)S(1)}, bf16[256,256]{1,0:T(8,128)(2,1)S(1)}, u32[]{:S(2)}, u32[]{:S(2)}) collective-permute-start(bf16[256,256]{1,0:T(8,128)(2,1)S(1)} %get-tuple-element.61), channel_id=1, source_target_pairs={{0,4},{1,5},{2,6},{3,7},{4,0},{5,1},{6,2},{7,3},{8,12},{9,13},{10,... | collective-permute-start | bytes 393224 | tf_op jit(solution)/shard_map/ppermute | solution.py:681
  77.3 0.9 %collective-permute-start.10 = (bf16[256,256]{1,0:T(8,128)(2,1)S(1)}, bf16[256,256]{1,0:T(8,128)(2,1)S(1)}, u32[]{:S(2)}, u32[]{:S(2)}) collective-permute-start(bf16[256,256]{1,0:T(8,128)(2,1)S(1)} %get-tuple-element.62), channel_id=1, source_target_pairs={{0,6},{1,7},{2,0},{3,1},{4,2},{5,3},{6,4},{7,5},{8,14},{9,15},{10,... | collective-permute-start | bytes 393224 | tf_op jit(solution)/shard_map/ppermute | solution.py:681
  78.2 4.9 %input_gradient.1 = bf16[2048,640]{1,0:T(8,128)(2,1)} custom-call(bf16[2048,640]{1,0:T(8,128)(2,1)} %get-tuple-element.48.gx_hbm, bf16[16,128,640]{2,1,0:T(8,128)(2,1)} %get-tuple-element.52.tst_hbm, bf16[2048,256]{1,0:T(8,128)(2,1)} %get-tuple-element.44.bc_hbm, bf16[2048,128]{1,0:T(8,128)(2,1)} %get-tuple-element.49.sc_hbm, bf16[256,640]{1,0:T(8,128)(2,1)S(1)} %bitcast.5, ...), custom_call_target="tpu_custom_call" | custom-call | flops 2000000000 | bytes 12000000 | tf_op jit(solution)/shard_map/input_gradient/pallas_call | solution.py:572
  83.2 0.2 collective-permute-done.9.c_ref
  83.4 0.3 collective-permute-done.10.d_ref
  83.6 0.7 totals.1
  (15 shorter events, 0.2 us)
Async XLA Ops:
  1.5 11.7 %collective-permute-start.2 = (bf16[256,256]{1,0:T(8,128)(2,1)S(1)}, bf16[256,256]{1,0:T(8,128)(2,1)S(1)}, u32[]{:S(2)}, u32[]{:S(2)}) collective-permute-start(bf16[256,256]{1,0:T(8,128)(2,1)S(1)} %join.1.m0), channel_id=1, source_target_pairs={{0,6},{1,7},{2,0},{3,1},{4,2},{5,3},{6,4},{7,5},{8,14},{9,15},{10,... | collective-permute-start | bytes 393224 | tf_op jit(solution)/shard_map/ppermute | solution.py:663
  5.2 8.1 %collective-permute-start.1 = (bf16[256,256]{1,0:T(8,128)(2,1)S(1)}, bf16[256,256]{1,0:T(8,128)(2,1)S(1)}, u32[]{:S(2)}, u32[]{:S(2)}) collective-permute-start(bf16[256,256]{1,0:T(8,128)(2,1)S(1)} %join.1.m0), channel_id=1, source_target_pairs={{0,4},{1,5},{2,6},{3,7},{4,0},{5,1},{6,2},{7,3},{8,12},{9,13},{10,... | collective-permute-start | bytes 393224 | tf_op jit(solution)/shard_map/ppermute | solution.py:663
  5.5 9.3 %collective-permute-start = (bf16[256,256]{1,0:T(8,128)(2,1)S(1)}, bf16[256,256]{1,0:T(8,128)(2,1)S(1)}, u32[]{:S(2)}, u32[]{:S(2)}) collective-permute-start(bf16[256,256]{1,0:T(8,128)(2,1)S(1)} %join.1.m0), channel_id=1, source_target_pairs={{0,2},{1,3},{2,4},{3,5},{4,6},{5,7},{6,0},{7,1},{8,10},{9,11},{10,... | collective-permute-start | bytes 393224 | tf_op jit(solution)/shard_map/ppermute | solution.py:663
  14.8 1.6 %collective-permute-start.3 = (bf16[256,256]{1,0:T(8,128)(2,1)S(1)}, bf16[256,256]{1,0:T(8,128)(2,1)S(1)}, u32[]{:S(2)}, u32[]{:S(2)}) collective-permute-start(bf16[256,256]{1,0:T(8,128)(2,1)S(1)} %join.1.m0), channel_id=1, source_target_pairs={{0,1},{1,0},{2,3},{3,2},{4,5},{5,4},{6,7},{7,6},{8,9},{9,8},{10,11... | collective-permute-start | bytes 393224 | tf_op jit(solution)/shard_map/ppermute | solution.py:668
  15.4 1.3 %collective-permute-start.4 = (bf16[256,256]{1,0:T(8,128)(2,1)S(1)}, bf16[256,256]{1,0:T(8,128)(2,1)S(1)}, u32[]{:S(2)}, u32[]{:S(2)}) collective-permute-start(bf16[256,256]{1,0:T(8,128)(2,1)S(1)} %collective-permute-done.m1), channel_id=1, source_target_pairs={{0,1},{1,0},{2,3},{3,2},{4,5},{5,4},{6,7},{7,6},{8,9},{9,8},{10,11... | collective-permute-start | bytes 393224 | tf_op jit(solution)/shard_map/ppermute | solution.py:668
  15.4 1.6 %collective-permute-start.5 = (bf16[256,256]{1,0:T(8,128)(2,1)S(1)}, bf16[256,256]{1,0:T(8,128)(2,1)S(1)}, u32[]{:S(2)}, u32[]{:S(2)}) collective-permute-start(bf16[256,256]{1,0:T(8,128)(2,1)S(1)} %collective-permute-done.1.m2), channel_id=1, source_target_pairs={{0,1},{1,0},{2,3},{3,2},{4,5},{5,4},{6,7},{7,6},{8,9},{9,8},{10,11... | collective-permute-start | bytes 393224 | tf_op jit(solution)/shard_map/ppermute | solution.py:668
  15.9 1.5 %collective-permute-start.6 = (bf16[256,256]{1,0:T(8,128)(2,1)S(1)}, bf16[256,256]{1,0:T(8,128)(2,1)}, u32[]{:S(2)}, u32[]{:S(2)}) collective-permute-start(bf16[256,256]{1,0:T(8,128)(2,1)S(1)} %collective-permute-done.2.m3), channel_id=1, source_target_pairs={{0,1},{1,0},{2,3},{3,2},{4,5},{5,4},{6,7},{7,6},{8,9},{9,8},{10,11... | collective-permute-start | bytes 393224 | tf_op jit(solution)/shard_map/ppermute | solution.py:668
  17.4 15.7 %copy-start.3 = (f32[10]{0:T(128)S(1)}, f32[10]{0:T(128)}, u32[]{:S(2)}) copy-start(f32[10]{0:T(128)} %param.15) | copy-start | bytes 124
  22.0 25.5 %all-to-all-start = ((bf16[32,8,768]{2,1,0:T(8,128)(2,1)}), bf16[32,8,768]{2,1,0:T(8,128)(2,1)S(1)}, u32[]{:S(2)}, u32[]{:S(2)}) async-start(bf16[32,8,768]{2,1,0:T(8,128)(2,1)} %get-tuple-element.43), calls=%async_computation | async-start | bytes 786432 | tf_op jit(solution)/shard_map/all_to_all | solution.py:670
  33.2 14.2 %copy-start = (bf16[128,640]{1,0:T(8,128)(2,1)S(1)}, bf16[128,640]{1,0:T(8,128)(2,1)}, u32[]{:S(2)}) copy-start(bf16[128,640]{1,0:T(8,128)(2,1)} %constant.21.clone.spf_ref.sp_ref) | copy-start | bytes 491524
  33.2 20.0 %copy-start.1 = (bf16[128,1280]{1,0:T(8,128)(2,1)S(1)}, bf16[128,1280]{1,0:T(8,128)(2,1)}, u32[]{:S(2)}) copy-start(bf16[128,1280]{1,0:T(8,128)(2,1)} %constant.20.clone.sp_ref) | copy-start | bytes 983044
  33.2 20.0 %copy-start.2 = (bf16[128,128]{1,0:T(8,128)(2,1)S(1)}, bf16[128,128]{1,0:T(8,128)(2,1)}, u32[]{:S(2)}) copy-start(bf16[128,128]{1,0:T(8,128)(2,1)} %get-tuple-element.42.dec_hbm.dec_ref) | copy-start | bytes 98308
  48.5 15.7 %all-to-all-start.1 = ((bf16[32,8,640]{2,1,0:T(8,128)(2,1)}), bf16[32,8,640]{2,1,0:T(8,128)(2,1)S(1)}, u32[]{:S(2)}, u32[]{:S(2)}) async-start(bf16[32,8,640]{2,1,0:T(8,128)(2,1)} %scan.1), calls=%async_computation.1 | async-start | bytes 655360 | tf_op jit(solution)/shard_map/all_to_all | solution.py:675
  68.5 5.4 %collective-permute-start.7 = (bf16[4,256,256]{2,1,0:T(8,128)(2,1)S(1)}, bf16[4,256,256]{2,1,0:T(8,128)(2,1)S(1)}, u32[]{:S(2)}, u32[]{:S(2)}) collective-permute-start(bf16[4,256,256]{2,1,0:T(8,128)(2,1)S(1)} %get-tuple-element.58), channel_id=1, source_target_pairs={{0,1},{1,0},{2,3},{3,2},{4,5},{5,4},{6,7},{7,6},{8,9},{9,8},{10,11... | collective-permute-start | bytes 1572872 | tf_op jit(solution)/shard_map/ppermute | solution.py:680
  74.6 8.6 %collective-permute-start.8 = (bf16[256,256]{1,0:T(8,128)(2,1)S(1)}, bf16[256,256]{1,0:T(8,128)(2,1)S(1)}, u32[]{:S(2)}, u32[]{:S(2)}) collective-permute-start(bf16[256,256]{1,0:T(8,128)(2,1)S(1)} %get-tuple-element.60), channel_id=1, source_target_pairs={{0,2},{1,3},{2,4},{3,5},{4,6},{5,7},{6,0},{7,1},{8,10},{9,11},{10,... | collective-permute-start | bytes 393224 | tf_op jit(solution)/shard_map/ppermute | solution.py:681
  75.7 7.6 %collective-permute-start.9 = (bf16[256,256]{1,0:T(8,128)(2,1)S(1)}, bf16[256,256]{1,0:T(8,128)(2,1)S(1)}, u32[]{:S(2)}, u32[]{:S(2)}) collective-permute-start(bf16[256,256]{1,0:T(8,128)(2,1)S(1)} %get-tuple-element.61), channel_id=1, source_target_pairs={{0,4},{1,5},{2,6},{3,7},{4,0},{5,1},{6,2},{7,3},{8,12},{9,13},{10,... | collective-permute-start | bytes 393224 | tf_op jit(solution)/shard_map/ppermute | solution.py:681
  77.3 6.3 %collective-permute-start.10 = (bf16[256,256]{1,0:T(8,128)(2,1)S(1)}, bf16[256,256]{1,0:T(8,128)(2,1)S(1)}, u32[]{:S(2)}, u32[]{:S(2)}) collective-permute-start(bf16[256,256]{1,0:T(8,128)(2,1)S(1)} %get-tuple-element.62), channel_id=1, source_target_pairs={{0,6},{1,7},{2,0},{3,1},{4,2},{5,3},{6,4},{7,5},{8,14},{9,15},{10,... | collective-permute-start | bytes 393224 | tf_op jit(solution)/shard_map/ppermute | solution.py:681
